TPU v7x, 32 devices: a whole 2x2x4 slice. The times are simulated.
32 devices in a mesh: group: 1, expert: 16 (over z, y, x), tensor: 2 (over core).
Axes of the slice: x: 2, y: 2, z: 4, core: 2. Of those that a mesh axis runs over, the one named last changes fastest.
Arguments:
- resid: bfloat16 [3072, 4096], P(('group', 'expert'), 'tensor'), as said below
- context: bfloat16 [3072, 4096], P(('group', 'expert')), may hold values from -6 to 6
- out_weight: bfloat16 [4096, 4096], P('expert', 'tensor'), may hold values from -0.09375 to 0.09375
- norm_gain: float32 [4096], replicated, may hold values from 0.1 to 1.9
- gate_up: bfloat16 [16, 2, 4096, 768], P('expert', None, None, 'tensor'), may hold values from -0.09375 to 0.09375
- down_weight: bfloat16 [16, 768, 4096], P('expert', None, 'tensor'), may hold values from -0.21875 to 0.21875
- expert_ids: int32 [3072, 8], P(('group', 'expert')), may hold values from 0 to 127, as said below
- slots: int32 [3072, 8], P(('group', 'expert')), may hold values from -1 to 23, as said below
- token_order: int32 [256, 24], P(('group', 'expert')), may hold values from -1 to 191, as said below
- combine: float32 [3072, 8], P(('group', 'expert')), may hold values from 0.1 to 0.6
Outputs:
- mixed: bfloat16 [3072, 4096], P(('group', 'expert'), 'tensor')
Inputs may be any that keep to these rules, and one draw needn't show every extreme that they name: `expert_ids`: each row names 8 different experts of the model's 128; only those under 16 are in flight. `slots`: for a choice of an expert in flight, its place among the rows that the token's index of expert sends to that expert, counted in order of token and then choice; -1 where the expert is not in flight or 24 rows came before it. `token_order`: row s * 16 + m holds, for each slot c, the token (numbered within index s) whose choice has expert m and slot c, or -1 where no choice has it; it agrees with expert_ids and slots. `resid`: rows of a few tokens to several features of order one; their scales differ from token to token and from feature to feature.
All inputs are finite; a program needn't handle non-finite values.
Results may differ from a plain program's by a relative error of at most 0.0043.
Values may be sent and summed in bfloat16 or wider, within the bound.
A program may use at most 128 MiB of HBM per device.

v0:
```python
import jax
import jax.numpy as jnp
from jax import lax
from jax.sharding import PartitionSpec as P

epsilon = 1e-06


def swapped(value, axis, stride):
    mask = 2**stride
    pairs = [(source, source ^ mask) for source in range(lax.axis_size(axis))]
    return lax.ppermute(value, axis, pairs)


def per_device(
    resid,
    context,
    out_weight,
    norm_gain,
    gate_up,
    down_weight,
    expert_ids,
    slots,
    token_order,
    combine,
):
    tok_rows = resid.shape[0]
    half_width = resid.shape[1]
    pair_side = lax.axis_index("tensor")
    attention = jnp.dot(
        context,
        lax.all_gather(out_weight, "expert", axis=0, tiled=True),
        preferred_element_type=jnp.float32,
    )
    hidden_state = (resid.astype(jnp.float32) + attention).astype(jnp.bfloat16)
    state_float = hidden_state.astype(jnp.float32)
    occupied = token_order >= 0
    pick_rows = jnp.where(occupied, token_order, 0)
    gate_weight = gate_up[0, 0]
    up_weight = gate_up[0, 1]
    down_part = down_weight[0]
    whole_rows = lax.all_gather(hidden_state, "tensor", axis=1, tiled=True)
    whole_float = whole_rows.astype(jnp.float32)
    row_scale = lax.rsqrt(jnp.mean(whole_float * whole_float, axis=1, keepdims=True) + epsilon)
    normed = (whole_float * row_scale * norm_gain).astype(jnp.bfloat16)
    packed = jnp.where(occupied[:, :, None], normed[pick_rows], jnp.zeros((), jnp.bfloat16))
    features = lax.all_to_all(packed, "expert", split_axis=0, concat_axis=0, tiled=True)
    sources = features.shape[0]
    slot_count = features.shape[1]
    flat_rows = features.reshape(sources * slot_count, features.shape[2])
    gate_part = jnp.dot(flat_rows, gate_weight, preferred_element_type=jnp.float32)
    up_part = jnp.dot(flat_rows, up_weight, preferred_element_type=jnp.float32)
    active = (jax.nn.silu(gate_part) * up_part).astype(jnp.bfloat16)
    partner = swapped(active, "tensor", 0)
    low_half = jnp.where(pair_side == 0, active, partner)
    high_half = jnp.where(pair_side == 0, partner, active)
    product = jnp.dot(
        jnp.concatenate([low_half, high_half], axis=1),
        down_part,
        preferred_element_type=jnp.float32,
    )
    product = product.astype(jnp.bfloat16).reshape(sources, slot_count, down_part.shape[1])
    returned = lax.all_to_all(product, "expert", split_axis=0, concat_axis=0, tiled=True)
    capacity = token_order.shape[1]
    live_slot = slots >= 0
    flat_index = jnp.where(live_slot, expert_ids * capacity + slots, 0)
    back_table = returned.reshape(-1, half_width)
    mixed_sum = jnp.zeros((tok_rows, half_width), jnp.float32)
    for column in range(expert_ids.shape[1]):
        got_rows = back_table[flat_index[:, column]].astype(jnp.float32)
        weight = jnp.where(live_slot[:, column], combine[:, column], jnp.zeros((), jnp.float32))
        mixed_sum = mixed_sum + weight[:, None] * got_rows
    return (state_float + mixed_sum).astype(jnp.bfloat16)


def solution(mesh):
    placed = (
        P(("group", "expert"), "tensor"),
        P(("group", "expert"), None),
        P("expert", "tensor"),
        P(),
        P("expert", None, None, "tensor"),
        P("expert", None, "tensor"),
        P(("group", "expert"), None),
        P(("group", "expert"), None),
        P(("group", "expert"), None),
        P(("group", "expert"), None),
    )
    return jax.shard_map(
        per_device,
        mesh=mesh,
        in_specs=placed,
        out_specs=P(("group", "expert"), "tensor"),
        check_vma=False,
    )
```

profile of v0, /device:TPU:7, one launch (start us, length us, event | category | flops | bytes accessed | tf_op | source)
XLA Modules:
  0.0 413.1 jit_solution(12520747809672607451)
XLA Ops:
  6.5 0.7 all-gather.3.cloned.1.call-update
  7.3 0.0 copy-start.3
  7.3 0.0 all-gather.5.cloned.1.call-start
  7.3 194.3 %all-gather.3.cloned.1.call-done = bf16[4096,2048]{1,0:T(8,128)(2,1)} async-done(((bf16[256,2048]{1,0:T(8,128)(2,1)}), bf16[4096,2048]{1,0:T(8,128)(2,1)}) %all-gather.3.cloned.1.call-update) | async-done | bytes 16777232 | tf_op jit(solution)/shard_map/all_gather | solution.py:32
  201.6 10.6 %fusion.14 = bf16[192,2048]{1,0:T(8,128)(2,1)} fusion(bf16[192,4096]{1,0:T(8,128)(2,1)} %param.11, bf16[4096,2048]{1,0:T(8,128)(2,1)} %all-gather.3.cloned.1.call-done, bf16[192,2048]{1,0:T(8,128)(2,1)} %param.10), kind=kOutput, calls=%fused_computation.25 | convolution fusion | flops 3222405120 | bytes 19922944 | tf_op jit(solution)/shard_map/dot_general | solution.py:30
  212.3 0.0 all-gather.5.cloned.1.call-update
  212.3 0.1 reshape.24
  212.5 10.1 %all-gather.5.cloned.1.call-done = bf16[192,4096]{1,0:T(8,128)(2,1)} async-done(((bf16[192,2048]{1,0:T(8,128)(2,1)}), bf16[192,4096]{1,0:T(8,128)(2,1)}) %all-gather.5.cloned.1.call-update) | async-done | bytes 1572880 | tf_op jit(solution)/shard_map/all_gather | solution.py:42
  222.5 1.9 fusion
  224.5 1.6 fusion.2
  226.1 9.9 %gather_fusion = bf16[384,4096]{1,0:T(8,128)(2,1)} fusion(bf16[192,4096]{1,0:T(8,128)(2,1)} %fusion.2, s32[1024]{0:T(1024)S(1)} %pad_clamp_fusion.8), kind=kCustom, calls=%fused_computation | custom fusion | bytes 6292992 | tf_op jit(solution)/shard_map/gather | solution.py:46
  235.9 2.2 broadcast_select_fusion
  238.1 0.0 slice-start
  238.1 74.8 %all_to_all.10 = bf16[16,24,4096]{2,1,0:T(8,128)(2,1)S(1)} all-to-all(bf16[16,24,4096]{2,1,0:T(8,128)(2,1)S(1)} %broadcast_select_fusion), channel_id=1, replica_groups=mesh['group'=1,'expert'=16,'tensor'=2] {'expert'}, dimensions={0} | all-to-all | bytes 6291456 | tf_op jit(solution)/shard_map/all_to_all | solution.py:47
  312.9 3.9 fusion.7
  316.9 1.8 fusion.18
  318.7 2.4 collective-permute-start
  321.1 1.3 collective-permute-done
  322.4 1.0 broadcast_select_fusion.2
  323.5 2.6 fusion.11
  326.1 5.9 %all-to-all-start.1 = ((bf16[16,24,2048]{2,1,0:T(8,128)(2,1)}), bf16[16,24,2048]{2,1,0:T(8,128)(2,1)}, u32[]{:S(2)}, u32[]{:S(2)}) async-start(bf16[16,24,2048]{2,1,0:T(8,128)(2,1)} %bitcast.40), calls=%async_computation.1 | async-start | bytes 3145728 | tf_op jit(solution)/shard_map/all_to_all | solution.py:63
  331.9 0.0 copy-done.2
  332.2 33.3 %all-to-all-done.1 = bf16[16,24,2048]{2,1,0:T(8,128)(2,1)} async-done(((bf16[16,24,2048]{2,1,0:T(8,128)(2,1)}), bf16[16,24,2048]{2,1,0:T(8,128)(2,1)}, u32[]{:S(2)}, u32[]{:S(2)}) %all-to-all-start.1) | async-done | bytes 1572896 | tf_op jit(solution)/shard_map/all_to_all | solution.py:63
  365.5 4.4 %gather_fusion.1 = bf16[192,2048]{1,0:T(8,128)(2,1)} fusion(bf16[384,2048]{1,0:T(8,128)(2,1)} %bitcast.7, s32[1024]{0:T(1024)S(1)} %pad_clamp_fusion.7), kind=kCustom, calls=%fused_computation.1 | custom fusion | bytes 1573632 | tf_op jit(solution)/shard_map/gather | solution.py:70
  369.9 4.4 %gather_fusion.2 = bf16[192,2048]{1,0:T(8,128)(2,1)} fusion(bf16[384,2048]{1,0:T(8,128)(2,1)} %bitcast.7, s32[1024]{0:T(1024)S(1)} %pad_clamp_fusion.6), kind=kCustom, calls=%fused_computation.2 | custom fusion | bytes 1573632 | tf_op jit(solution)/shard_map/gather | solution.py:70
  374.3 4.4 %gather_fusion.3 = bf16[192,2048]{1,0:T(8,128)(2,1)} fusion(bf16[384,2048]{1,0:T(8,128)(2,1)} %bitcast.7, s32[1024]{0:T(1024)S(1)} %pad_clamp_fusion.5), kind=kCustom, calls=%fused_computation.3 | custom fusion | bytes 1573632 | tf_op jit(solution)/shard_map/gather | solution.py:70
  378.7 4.4 %gather_fusion.4 = bf16[192,2048]{1,0:T(8,128)(2,1)} fusion(bf16[384,2048]{1,0:T(8,128)(2,1)} %bitcast.7, s32[1024]{0:T(1024)S(1)} %pad_clamp_fusion.4), kind=kCustom, calls=%fused_computation.4 | custom fusion | bytes 1573632 | tf_op jit(solution)/shard_map/gather | solution.py:70
  383.1 4.4 %gather_fusion.5 = bf16[192,2048]{1,0:T(8,128)(2,1)} fusion(bf16[384,2048]{1,0:T(8,128)(2,1)} %bitcast.7, s32[1024]{0:T(1024)S(1)} %pad_clamp_fusion.3), kind=kCustom, calls=%fused_computation.5 | custom fusion | bytes 1573632 | tf_op jit(solution)/shard_map/gather | solution.py:70
  387.5 4.4 %gather_fusion.6 = bf16[192,2048]{1,0:T(8,128)(2,1)} fusion(bf16[384,2048]{1,0:T(8,128)(2,1)} %bitcast.7, s32[1024]{0:T(1024)S(1)} %pad_clamp_fusion.2), kind=kCustom, calls=%fused_computation.6 | custom fusion | bytes 1573632 | tf_op jit(solution)/shard_map/gather | solution.py:70
  391.9 4.4 %gather_fusion.7 = bf16[192,2048]{1,0:T(8,128)(2,1)} fusion(bf16[384,2048]{1,0:T(8,128)(2,1)} %bitcast.7, s32[1024]{0:T(1024)S(1)} %pad_clamp_fusion.1), kind=kCustom, calls=%fused_computation.7 | custom fusion | bytes 1573632 | tf_op jit(solution)/shard_map/gather | solution.py:70
  396.4 4.6 %gather_fusion.8 = bf16[192,2048]{1,0:T(8,128)(2,1)} fusion(bf16[384,2048]{1,0:T(8,128)(2,1)} %bitcast.7, s32[1024]{0:T(1024)S(1)} %pad_clamp_fusion), kind=kCustom, calls=%fused_computation.8 | custom fusion | bytes 1573632 | tf_op jit(solution)/shard_map/gather | solution.py:70
  401.0 5.3 %add_convert_fusion = bf16[192,2048]{1,0:T(8,128)(2,1)} fusion(bf16[192,2048]{1,0:T(8,128)(2,1)} %gather_fusion.8, bf16[192,2048]{1,0:T(8,128)(2,1)} %gather_fusion.7, bf16[192,2048]{1,0:T(8,128)(2,1)} %gather_fusion.6, bf16[192,2048]{1,0:T(8,128)(2,1)} %gather_fusion.5, bf16[192,2048]{1,0:T(8,128)(2,1)} %gather_fusion.4, ...), kind=kLoop, calls=%fused_computation.26 | loop fusion | flops 10223616 | bytes 7870464 | tf_op jit(solution)/shard_map/convert_element_type | solution.py:73
  (33 shorter events, 0.1 us)
Async XLA Ops:
  6.5 316.9 %copy-start = (bf16[1,768,2048]{2,1,0:T(8,128)(2,1)S(1)}, bf16[1,768,2048]{2,1,0:T(8,128)(2,1)}, u32[]{:S(2)}) copy-start(bf16[1,768,2048]{2,1,0:T(8,128)(2,1)} %param.15) | copy-start | bytes 9437188
  6.5 195.1 %all-gather.3.cloned.1.call-start = ((), (), s32[]{:S(2)}) async-start(), calls=%async_computation.2 | async-start | bytes 17825792 | tf_op jit(solution)/shard_map/all_gather | solution.py:32
  7.3 205.1 %copy-start.3 = (s32[16,24]{1,0:T(8,128)S(1)}, s32[16,24]{1,0:T(8,128)}, u32[]{:S(2)}) copy-start(s32[16,24]{1,0:T(8,128)} %param.18) | copy-start | bytes 4612
  7.3 215.2 %all-gather.5.cloned.1.call-start = ((), (), s32[]{:S(2)}) async-start(), calls=%async_computation.3 | async-start | bytes 2359296 | tf_op jit(solution)/shard_map/all_gather | solution.py:42
  212.3 12.2 %copy-start.4 = (f32[4096]{0:T(1024)S(1)}, f32[4096]{0:T(1024)}, u32[]{:S(2)}) copy-start(f32[4096]{0:T(1024)} %param.13) | copy-start | bytes 49156
  222.5 1.9 copy-start.1
  238.1 78.7 %slice-start = ((s8[6291456]{0:T(1024)(128)(4,1)}), s8[4194304]{0:T(1024)(128)(4,1)S(1)}, s32[]{:S(2)}) async-start(s8[6291456]{0:T(1024)(128)(4,1)} %bitcast.59), calls=%async_computation.4 | async-start | bytes 8388608
  312.9 3.9 slice-start.1
  318.7 3.7 collective-permute-start
  326.1 5.9 %copy-start.2 = (s32[192,8]{0,1:T(8,128)S(1)}, s32[192,8]{0,1:T(8,128)}, u32[]{:S(2)}) copy-start(s32[192,8]{0,1:T(8,128)} %param.17) | copy-start | bytes 18436
  326.1 5.9 %copy-start.5 = (s32[192,8]{0,1:T(8,128)S(1)}, s32[192,8]{0,1:T(8,128)}, u32[]{:S(2)}) copy-start(s32[192,8]{0,1:T(8,128)} %param.16) | copy-start | bytes 18436
  326.1 6.1 %copy-start.6 = (f32[192,8]{0,1:T(8,128)S(1)}, f32[192,8]{0,1:T(8,128)}, u32[]{:S(2)}) copy-start(f32[192,8]{0,1:T(8,128)} %param.19) | copy-start | bytes 18436
  326.1 39.4 %all-to-all-start.1 = ((bf16[16,24,2048]{2,1,0:T(8,128)(2,1)}), bf16[16,24,2048]{2,1,0:T(8,128)(2,1)}, u32[]{:S(2)}, u32[]{:S(2)}) async-start(bf16[16,24,2048]{2,1,0:T(8,128)(2,1)} %bitcast.40), calls=%async_computation.1 | async-start | bytes 3145728 | tf_op jit(solution)/shard_map/all_to_all | solution.py:63
Sparse Core Ops, SparseCore 0:
  10.1 191.4 all-gather.2
  212.4 10.0 all-gather.4
where the time goes:
time: 418 us; the launch traced here: 413 us
  waiting for transfers between devices  240 us (57%)
  blocking collectives  74.8 us (18%)
  local copies, waits for them, and re-layouts  45.5 us (11%)
  matrix products  19 us (5%)
  between operations  13.6 us (3%)
  other arithmetic  12.1 us (3%)
  starting transfers between devices  8.32 us (2%)
    all_gather x1, waiting for transfers between devices, per_device(): lax.all_gather(out_weight, 'expert', axis=0, tiled=True)  194 us
    all_to_all x1, blocking collectives, per_device(): lax.all_to_all(packed, 'expert', split_axis=0, concat_axis=0, tiled=True)  74.8 us
    gather x8, local copies, waits for them, and re-layouts, per_device(): got_rows = back_table[flat_index[:, column]].astype(jnp.float32)  35.5 us
    all_to_all x1, waiting for transfers between devices, per_device(): lax.all_to_all(product, 'expert', split_axis=0, concat_axis=0, tiled=True)  33.3 us
    dot_general x1, matrix products, per_device(): jnp.dot(context, lax.all_gather(out_weight, 'expert', axis=0, tiled=True)...  10.6 us
    all_gather x1, waiting for transfers between devices, per_device(): whole_rows = lax.all_gather(hidden_state, 'tensor', axis=1, tiled=True)  10.1 us
    gather x1, local copies, waits for them, and re-layouts, per_device(): normed[pick_rows]  9.86 us
  transfers between devices with their start and end apart: 4, of which 4 were waited for; matrix products, arithmetic and copies ran while one was open for 0% of the time, Pallas kernels for 0%

commit v1 on v0

v1 whole, which is shorter than its diff:
```python
import jax
import jax.numpy as jnp
from jax import lax
from jax.sharding import PartitionSpec as P

epsilon = 1e-06


def per_device(
    resid,
    context,
    out_weight,
    norm_gain,
    gate_up,
    down_weight,
    expert_ids,
    slots,
    token_order,
    combine,
):
    tok_rows, half_width = resid.shape
    members = lax.axis_size("expert")
    near = 4
    far = members // near
    planes = [[p * near + i for i in range(near)] for p in range(far)]
    lines = [[p * near + i for p in range(far)] for i in range(near)]
    pair_side = lax.axis_index("tensor")
    k_rows = out_weight.shape[0]
    plane_weight = lax.all_gather(out_weight, "expert", axis=0, tiled=True, axis_index_groups=planes)
    context_parts = context.reshape(tok_rows, far, near * k_rows).transpose(1, 0, 2)
    line_context = lax.all_to_all(
        context_parts, "expert", split_axis=0, concat_axis=0, tiled=True, axis_index_groups=lines
    )
    partial = jnp.dot(
        line_context.reshape(far * tok_rows, near * k_rows), plane_weight, preferred_element_type=jnp.float32
    ).astype(jnp.bfloat16)
    parts = lax.all_to_all(
        partial.reshape(far, tok_rows, half_width),
        "expert",
        split_axis=0,
        concat_axis=0,
        tiled=True,
        axis_index_groups=lines,
    )
    attention = jnp.sum(parts.astype(jnp.float32), axis=0)
    hidden_state = (resid.astype(jnp.float32) + attention).astype(jnp.bfloat16)
    state_float = hidden_state.astype(jnp.float32)
    width = norm_gain.shape[0]
    squares = lax.psum(jnp.sum(state_float * state_float, axis=1, keepdims=True), "tensor")
    row_scale = lax.rsqrt(squares / width + epsilon)
    gain = lax.dynamic_slice_in_dim(norm_gain, pair_side * half_width, half_width)
    normed = (state_float * row_scale * gain).astype(jnp.bfloat16)
    capacity = token_order.shape[1]
    tokens = jnp.arange(tok_rows, dtype=jnp.int32)
    pick = (token_order.reshape(-1, 1) == tokens[None, :]).astype(jnp.bfloat16)
    packed = jnp.dot(pick, normed, preferred_element_type=jnp.float32).astype(jnp.bfloat16)
    packed = packed.reshape(members, capacity, half_width)
    features = lax.all_to_all(packed, "expert", split_axis=0, concat_axis=0, tiled=True)
    flat_rows = features.reshape(members * capacity, half_width)
    flat_rows = lax.all_gather(flat_rows, "tensor", axis=1, tiled=True)
    gate_part = jnp.dot(flat_rows, gate_up[0, 0], preferred_element_type=jnp.float32)
    up_part = jnp.dot(flat_rows, gate_up[0, 1], preferred_element_type=jnp.float32)
    active = (jax.nn.silu(gate_part) * up_part).astype(jnp.bfloat16)
    active = lax.all_gather(active, "tensor", axis=1, tiled=True)
    product = jnp.dot(active, down_weight[0], preferred_element_type=jnp.float32)
    product = product.astype(jnp.bfloat16).reshape(members, capacity, half_width)
    returned = lax.all_to_all(product, "expert", split_axis=0, concat_axis=0, tiled=True)
    flat_index = jnp.where(slots >= 0, expert_ids * capacity + slots, -1)
    places = jnp.arange(members * capacity, dtype=jnp.int32)
    weights = jnp.zeros((tok_rows, members * capacity), jnp.float32)
    for column in range(expert_ids.shape[1]):
        weights = weights + jnp.where(flat_index[:, column, None] == places[None, :], combine[:, column, None], 0.0)
    high = lax.reduce_precision(weights, 8, 7)
    middle = lax.reduce_precision(weights - high, 8, 7)
    low = weights - high - middle
    table = returned.reshape(-1, half_width)
    three = jnp.concatenate([high, middle, low], axis=0).astype(jnp.bfloat16)
    sums = jnp.dot(three, table, preferred_element_type=jnp.float32)
    mixed_sum = jnp.sum(sums.reshape(3, tok_rows, half_width), axis=0)
    return (state_float + mixed_sum).astype(jnp.bfloat16)


def solution(mesh):
    placed = (
        P(("group", "expert"), "tensor"),
        P(("group", "expert"), None),
        P("expert", "tensor"),
        P(),
        P("expert", None, None, "tensor"),
        P("expert", None, "tensor"),
        P(("group", "expert"), None),
        P(("group", "expert"), None),
        P(("group", "expert"), None),
        P(("group", "expert"), None),
    )
    return jax.shard_map(
        per_device,
        mesh=mesh,
        in_specs=placed,
        out_specs=P(("group", "expert"), "tensor"),
        check_vma=False,
    )
```

time: 418 us -> 277 us (0.66)
  waiting for transfers between devices: 240 us -> 125 us
  local copies, waits for them, and re-layouts: 45.5 us -> 6.14 us
  blocking collectives: 74.8 us -> 85.3 us
  other arithmetic: 12.1 us -> 6.38 us
  matrix products: 19 us -> 23.7 us
    all_gather x2, waiting for transfers between devices: 204 us -> 22.8 us  [the longest x1 14.5 us: per_device(): flat_rows = lax.all_gather(flat_rows, 'tensor', axis=1, tiled=True)]
    all_to_all x0 -> x1, waiting for transfers between devices: none -> 70.1 us  [per_device(): lax.all_to_all(partial.reshape(far, tok_rows, half_width), 'expert', spli...]
    gather x9 -> x0, local copies, waits for them, and re-layouts: 45.3 us -> none  [the longest x8 35.5 us: per_device(): got_rows = back_table[flat_index[:, column]].astype(jnp.float32)]
    all_to_all x0 -> x1, blocking collectives: none -> 40.6 us  [per_device(): lax.all_to_all(context_parts, 'expert', split_axis=0, concat_axis=0, tile...]
    all_to_all x1, blocking collectives: 74.8 us -> 39 us  [per_device(): lax.all_to_all(packed, 'expert', split_axis=0, concat_axis=0, tiled=True)]
    all_to_all x0 -> x1, starting transfers between devices: none -> 4.78 us  [per_device(): lax.all_to_all(partial.reshape(far, tok_rows, half_width), 'expert', spli...]
    dot_general x4 -> x6, matrix products: 19 us -> 23.7 us  [the longest x1 7.77 us: per_device(): jnp.dot(line_context.reshape(far * tok_rows, near * k_rows), plane_weight...]
    convert_element_type x1, other arithmetic: 5.28 us -> 1.06 us  [per_device(): return (state_float + mixed_sum).astype(jnp.bfloat16)]
  transfers between devices with their start and end apart: 4 -> 4, of which waited for: 4 -> 4; matrix products, arithmetic and copies ran while one was open for 0% -> 3% of each run, Pallas kernels for 0% -> 0%
where the time goes in v1:
time: 277 us; the launch traced here: 272 us
  waiting for transfers between devices  125 us (45%)
  blocking collectives  85.3 us (31%)
  matrix products  23.7 us (9%)
  between operations  13.6 us (5%)
  starting transfers between devices  11.4 us (4%)
  other arithmetic  6.38 us (2%)
  local copies, waits for them, and re-layouts  6.14 us (2%)
    all_to_all x1, waiting for transfers between devices, per_device(): lax.all_to_all(partial.reshape(far, tok_rows, half_width), 'expert', spli...  70.1 us
    all_to_all x1, blocking collectives, per_device(): lax.all_to_all(context_parts, 'expert', split_axis=0, concat_axis=0, tile...  40.6 us
    all_to_all x1, blocking collectives, per_device(): lax.all_to_all(packed, 'expert', split_axis=0, concat_axis=0, tiled=True)  39 us
    all_to_all x1, waiting for transfers between devices, per_device(): lax.all_to_all(product, 'expert', split_axis=0, concat_axis=0, tiled=True)  31.8 us
    all_gather x1, waiting for transfers between devices, per_device(): flat_rows = lax.all_gather(flat_rows, 'tensor', axis=1, tiled=True)  14.5 us
    all_gather x1, waiting for transfers between devices, per_device(): lax.all_gather(out_weight, 'expert', axis=0, tiled=True, axis_index_group...  8.34 us
    dot_general x1, matrix products, per_device(): jnp.dot(line_context.reshape(far * tok_rows, near * k_rows), plane_weight...  7.77 us
    all_to_all x1, starting transfers between devices, per_device(): lax.all_to_all(product, 'expert', split_axis=0, concat_axis=0, tiled=True)  6.56 us
  transfers between devices with their start and end apart: 4, of which 4 were waited for; matrix products, arithmetic and copies ran while one was open for 3% of the time, Pallas kernels for 0%

profile of v1, /device:TPU:7, one launch (start us, length us, event | category | flops | bytes accessed | tf_op | source)
XLA Modules:
  0.0 271.9 jit_solution(4799722090867612062)
XLA Ops:
  6.5 0.0 copy-start
  6.5 0.0 all-gather.3.cloned.1.call-start
  6.5 0.7 all-gather.3.cloned.1.call-update
  7.3 4.1 %reshape.34 = bf16[192,4,1024]{2,1,0:T(4,128)(2,1)} reshape(bf16[192,4096]{1,0:T(8,128)(2,1)} %param.11) | data formatting | bytes 3145728 | tf_op jit(solution)/shard_map/reshape | solution.py:30
  11.4 1.9 copy.12
  13.3 40.6 %all_to_all.20 = bf16[4,192,1024]{2,1,0:T(8,128)(2,1)} all-to-all(bf16[4,192,1024]{2,1,0:T(8,128)(2,1)S(1)} %copy.12), channel_id=1, replica_groups={{0,8,16,24},{2,10,18,26},{4,12,20,28},{6,14,22,30},{1,9,17,25},{3,11,19..., dimensions={0} | all-to-all | bytes 3145728 | tf_op jit(solution)/shard_map/all_to_all | solution.py:31
  53.9 8.3 %all-gather.3.cloned.1.call-done = bf16[1024,2048]{1,0:T(8,128)(2,1)} async-done(((bf16[256,2048]{1,0:T(8,128)(2,1)}), bf16[1024,2048]{1,0:T(8,128)(2,1)}) %all-gather.3.cloned.1.call-update) | async-done | bytes 4194320 | tf_op jit(solution)/shard_map/all_gather | solution.py:29
  62.2 7.8 %convolution_convert_fusion = bf16[768,2048]{1,0:T(8,128)(2,1)} fusion(bf16[768,1024]{1,0:T(8,128)(2,1)} %bitcast.55, bf16[1024,2048]{1,0:T(8,128)(2,1)} %all-gather.3.cloned.1.call-done), kind=kOutput, calls=%fused_computation.1 | convolution fusion | flops 3222798336 | bytes 8912896 | tf_op jit(solution)/shard_map/dot_general | solution.py:34
  70.0 4.8 %all-to-all-start.1 = ((bf16[4,192,2048]{2,1,0:T(8,128)(2,1)}), bf16[4,192,2048]{2,1,0:T(8,128)(2,1)}, u32[]{:S(2)}, u32[]{:S(2)}) async-start(bf16[4,192,2048]{2,1,0:T(8,128)(2,1)} %bitcast.53), calls=%async_computation.1 | async-start | bytes 6291456 | tf_op jit(solution)/shard_map/all_to_all | solution.py:37
  74.8 0.0 all-gather.5.cloned.1.call-start
  74.8 0.0 copy-done.5
  74.8 0.1 eq.167
  74.9 0.0 dynamic-slice-start
  74.9 70.1 %all-to-all-done.1 = bf16[4,192,2048]{2,1,0:T(8,128)(2,1)} async-done(((bf16[4,192,2048]{2,1,0:T(8,128)(2,1)}), bf16[4,192,2048]{2,1,0:T(8,128)(2,1)}, u32[]{:S(2)}, u32[]{:S(2)}) %all-to-all-start.1) | async-done | bytes 3145760 | tf_op jit(solution)/shard_map/all_to_all | solution.py:37
  145.0 2.7 %convert_reduce_fusion = f32[192,2048]{1,0:T(8,128)S(1)} fusion(bf16[4,192,2048]{2,1,0:T(8,128)(2,1)} %all-to-all-done.1), kind=kLoop, calls=%fused_computation | loop fusion | flops 2752512 | bytes 4718592 | tf_op jit(solution)/shard_map/reduce_sum | solution.py:45
  147.8 1.1 fusion.11
  148.9 3.5 %psum.7 = f32[192,1]{0,1:T(1,128)S(1)} all-reduce(f32[192,1]{0,1:T(1,128)S(1)} %bitcast.74), channel_id=1, replica_groups=mesh['group'=1,'expert'=16,'tensor'=2] {'tensor'}, use_global_device_ids=true, to_apply=%region_2.0 | all-reduce | flops 192 | bytes 1536 | tf_op jit(solution)/shard_map/psum | solution.py:49
  152.4 1.8 convolution_convert_fusion.1
  154.3 39.0 %all_to_all.21 = bf16[16,24,2048]{2,1,0:T(8,128)(2,1)} all-to-all(bf16[16,24,2048]{2,1,0:T(8,128)(2,1)S(1)} %bitcast.51), channel_id=1, replica_groups=mesh['group'=1,'expert'=16,'tensor'=2] {'expert'}, dimensions={0} | all-to-all | bytes 3145728 | tf_op jit(solution)/shard_map/all_to_all | solution.py:58
  193.2 0.0 all-gather.5.cloned.1.call-update
  193.3 14.5 %all-gather.5.cloned.1.call-done = bf16[384,4096]{1,0:T(8,128)(2,1)} async-done(((bf16[384,2048]{1,0:T(8,128)(2,1)}), bf16[384,4096]{1,0:T(8,128)(2,1)}) %all-gather.5.cloned.1.call-update) | async-done | bytes 3145744 | tf_op jit(solution)/shard_map/all_gather | solution.py:60
  207.7 4.8 %fusion.4 = f32[384,384]{1,0:T(8,128)S(1)} fusion(bf16[384,4096]{1,0:T(8,128)(2,1)} %all-gather.5.cloned.1.call-done, bf16[1,2,4096,384]{3,2,1,0:T(8,128)(2,1)} %param.14), kind=kOutput, calls=%fused_computation.6 | convolution fusion | flops 1207959552 | bytes 6881280 | tf_op jit(solution)/shard_map/dot_general | solution.py:61
  212.5 3.7 %fusion.18 = bf16[384,384]{1,0:T(8,128)(2,1)S(1)} fusion(bf16[384,4096]{1,0:T(8,128)(2,1)S(1)} %copy-done.7, bf16[1,2,4096,384]{3,2,1,0:T(8,128)(2,1)} %param.14, f32[384,384]{1,0:T(8,128)S(1)} %fusion.4), kind=kOutput, calls=%fused_computation.22 | convolution fusion | flops 1208844288 | bytes 7176192 | tf_op jit(solution)/shard_map/dot_general | solution.py:62
  216.2 2.2 all_gather.11
  218.5 2.6 fusion.8
  221.0 6.6 %all-to-all-start.3 = ((bf16[16,24,2048]{2,1,0:T(8,128)(2,1)}), bf16[16,24,2048]{2,1,0:T(8,128)(2,1)}, u32[]{:S(2)}, u32[]{:S(2)}) async-start(bf16[16,24,2048]{2,1,0:T(8,128)(2,1)} %bitcast.54), calls=%async_computation.3 | async-start | bytes 3145728 | tf_op jit(solution)/shard_map/all_to_all | solution.py:67
  227.6 0.0 copy-done.6
  227.7 0.6 reduce-precision_convert_fusion.1
  228.3 0.8 pad_maximum_fusion
  229.1 31.8 %all-to-all-done.3 = bf16[16,24,2048]{2,1,0:T(8,128)(2,1)} async-done(((bf16[16,24,2048]{2,1,0:T(8,128)(2,1)}), bf16[16,24,2048]{2,1,0:T(8,128)(2,1)}, u32[]{:S(2)}, u32[]{:S(2)}) %all-to-all-start.3) | async-done | bytes 1572896 | tf_op jit(solution)/shard_map/all_to_all | solution.py:67
  260.9 3.1 %convolution_reduce_fusion = f32[192,2048]{1,0:T(8,128)S(1)} fusion(bf16[3,192,384]{2,1,0:T(8,128)(2,1)} %bitcast.56, bf16[384,2048,1]{1,0,2:T(8,128)(2,1)} %bitcast.29), kind=kOutput, calls=%fused_computation.15 | convolution fusion | flops 906756096 | bytes 3588096 | tf_op jit(solution)/shard_map/dot_general | solution.py:78
  264.0 1.1 fusion.14
  (18 shorter events, 0.1 us)
Async XLA Ops:
  6.5 211.9 %copy-start = (bf16[1,768,2048]{2,1,0:T(8,128)(2,1)S(1)}, bf16[1,768,2048]{2,1,0:T(8,128)(2,1)}, u32[]{:S(2)}) copy-start(bf16[1,768,2048]{2,1,0:T(8,128)(2,1)} %param.15) | copy-start | bytes 9437188
  6.5 55.7 %all-gather.3.cloned.1.call-start = ((), (), s32[]{:S(2)}) async-start(), calls=%async_computation.4 | async-start | bytes 5242880 | tf_op jit(solution)/shard_map/all_gather | solution.py:29
  70.0 4.8 %copy-start.5 = (s32[16,24]{1,0:T(8,128)S(1)}, s32[16,24]{1,0:T(8,128)}, u32[]{:S(2)}) copy-start(s32[16,24]{1,0:T(8,128)} %param.18) | copy-start | bytes 4612
  70.0 75.0 %all-to-all-start.1 = ((bf16[4,192,2048]{2,1,0:T(8,128)(2,1)}), bf16[4,192,2048]{2,1,0:T(8,128)(2,1)}, u32[]{:S(2)}, u32[]{:S(2)}) async-start(bf16[4,192,2048]{2,1,0:T(8,128)(2,1)} %bitcast.53), calls=%async_computation.1 | async-start | bytes 6291456 | tf_op jit(solution)/shard_map/all_to_all | solution.py:37
  74.8 133.0 %all-gather.5.cloned.1.call-start = ((), (), s32[]{:S(2)}) async-start(), calls=%async_computation.5 | async-start | bytes 4718592 | tf_op jit(solution)/shard_map/all_gather | solution.py:60
  74.9 77.5 %dynamic-slice-start = ((f32[4096]{0:T(1024)}, s32[]{:T(128)}), f32[2048]{0:T(1024)S(1)}, s32[]{:S(2)}) async-start(f32[4096]{0:T(1024)} %param.13, s32[]{:T(128)} %select_n.41), calls=%async_computation.6 | async-start | bytes 16896 | tf_op jit(solution)/shard_map/dynamic_slice | solution.py:51
  145.0 2.8 %copy-start.2 = (bf16[192,2048]{1,0:T(8,128)(2,1)S(1)}, bf16[192,2048]{1,0:T(8,128)(2,1)}, u32[]{:S(2)}) copy-start(bf16[192,2048]{1,0:T(8,128)(2,1)} %param.10) | copy-start | bytes 2359300
  207.7 4.8 %copy-start.7 = (bf16[384,4096]{1,0:T(8,128)(2,1)S(1)}, bf16[384,4096]{1,0:T(8,128)(2,1)}, u32[]{:S(2)}) copy-start(bf16[384,4096]{1,0:T(8,128)(2,1)} %all-gather.5.cloned.1.call-done) | copy-start | bytes 9437188
  221.0 6.6 %copy-start.6 = (f32[192,8]{0,1:T(8,128)S(1)}, f32[192,8]{0,1:T(8,128)}, u32[]{:S(2)}) copy-start(f32[192,8]{0,1:T(8,128)} %param.19) | copy-start | bytes 18436
  221.0 6.6 %copy-start.3 = (s32[192,8]{0,1:T(8,128)S(1)}, s32[192,8]{0,1:T(8,128)}, u32[]{:S(2)}) copy-start(s32[192,8]{0,1:T(8,128)} %param.17) | copy-start | bytes 18436
  221.0 6.6 %copy-start.4 = (s32[192,8]{0,1:T(8,128)S(1)}, s32[192,8]{0,1:T(8,128)}, u32[]{:S(2)}) copy-start(s32[192,8]{0,1:T(8,128)} %param.16) | copy-start | bytes 18436
  221.0 39.9 %all-to-all-start.3 = ((bf16[16,24,2048]{2,1,0:T(8,128)(2,1)}), bf16[16,24,2048]{2,1,0:T(8,128)(2,1)}, u32[]{:S(2)}, u32[]{:S(2)}) async-start(bf16[16,24,2048]{2,1,0:T(8,128)(2,1)} %bitcast.54), calls=%async_computation.3 | async-start | bytes 3145728 | tf_op jit(solution)/shard_map/all_to_all | solution.py:67
  260.9 3.1 %copy-start.1 = (bf16[192,2048]{1,0:T(8,128)(2,1)S(1)}, bf16[192,2048]{1,0:T(8,128)(2,1)}, u32[]{:S(2)}) copy-start(bf16[192,2048]{1,0:T(8,128)(2,1)} %get-tuple-element.6) | copy-start | bytes 2359300
Sparse Core Ops, SparseCore 0:
  9.2 52.9 all-gather.2
  193.4 14.3 all-gather.4

commit v2 on v1

--- a/solution.py
+++ b/solution.py
@@ -1,9 +1,296 @@
+import functools
+
 import jax
 import jax.numpy as jnp
 from jax import lax
+from jax.experimental import pallas as pl
+from jax.experimental.pallas import tpu as pltpu
 from jax.sharding import PartitionSpec as P
 
 epsilon = 1e-06
+near = 4
+chunks = 4
+
+
+def attention_kernel(
+    members,
+    resid,
+    context,
+    weight,
+    hidden,
+    plane_weight,
+    line_context,
+    sums,
+    outgoing,
+    from_left,
+    from_right,
+    own_sem,
+    weight_send,
+    weight_recv,
+    context_send,
+    context_recv,
+    share_send,
+    share_recv,
+    chain_send,
+    left_recv,
+    right_recv,
+):
+    far = members // near
+    me = lax.axis_index("expert")
+    side = lax.axis_index("tensor")
+    line = lax.div(me, near)
+    spot = lax.rem(me, near)
+    rows, half = resid.shape
+    depth = weight.shape[0]
+    span = near * depth
+    piece = span // 2
+    wide = half // chunks
+
+    def columns(c):
+        return pl.ds(pl.multiple_of(c * wide, wide), wide)
+
+    def token_rows(q):
+        return pl.ds(pl.multiple_of(q * rows, rows), rows)
+
+    own_columns = pl.ds(pl.multiple_of(side * piece, piece), piece)
+
+    def weight_copy(d, c):
+        slot = pl.ds(pl.multiple_of(spot * depth, depth), depth)
+        return pltpu.make_async_remote_copy(
+            src_ref=weight.at[:, columns(c)],
+            dst_ref=plane_weight.at[slot, columns(c)],
+            send_sem=weight_send.at[d, c],
+            recv_sem=weight_recv.at[d, c],
+            device_id={"expert": line * near + lax.bitwise_xor(spot, d)},
+            device_id_type=pl.DeviceIdType.MESH,
+        )
+
+    def context_copy(d):
+        target = lax.rem(line + d, far)
+        return pltpu.make_async_remote_copy(
+            src_ref=context.at[:, pl.ds(pl.multiple_of(target * span + side * piece, piece), piece)],
+            dst_ref=line_context.at[token_rows(line), own_columns],
+            send_sem=context_send.at[d],
+            recv_sem=context_recv.at[d],
+            device_id={"expert": target * near + spot},
+            device_id_type=pl.DeviceIdType.MESH,
+        )
+
+    def share_copy(d):
+        place = line_context.at[token_rows(lax.rem(line - d + far, far)), own_columns]
+        return pltpu.make_async_remote_copy(
+            src_ref=place,
+            dst_ref=place,
+            send_sem=share_send.at[d],
+            recv_sem=share_recv.at[d],
+            device_id={"tensor": 1 - side},
+            device_id_type=pl.DeviceIdType.MESH,
+        )
+
+    def right_copy(q, c):
+        return pltpu.make_async_remote_copy(
+            src_ref=outgoing.at[token_rows(q), columns(c)],
+            dst_ref=from_left.at[token_rows(q), columns(c)],
+            send_sem=chain_send.at[q, c],
+            recv_sem=left_recv.at[q, c],
+            device_id={"expert": me + near},
+            device_id_type=pl.DeviceIdType.MESH,
+        )
+
+    def left_copy(q, c):
+        return pltpu.make_async_remote_copy(
+            src_ref=outgoing.at[token_rows(q), columns(c)],
+            dst_ref=from_right.at[token_rows(q), columns(c)],
+            send_sem=chain_send.at[q, c],
+            recv_sem=right_recv.at[q, c],
+            device_id={"expert": me - near},
+            device_id_type=pl.DeviceIdType.MESH,
+        )
+
+    barrier = pltpu.get_barrier_semaphore()
+    for d in range(1, near):
+        pl.semaphore_signal(
+            barrier,
+            inc=1,
+            device_id={"expert": line * near + lax.bitwise_xor(spot, d)},
+            device_id_type=pl.DeviceIdType.MESH,
+        )
+    for d in range(1, far):
+        pl.semaphore_signal(
+            barrier,
+            inc=1,
+            device_id={"expert": lax.rem(line + d, far) * near + spot},
+            device_id_type=pl.DeviceIdType.MESH,
+        )
+    pl.semaphore_signal(barrier, inc=1, device_id={"tensor": 1 - side}, device_id_type=pl.DeviceIdType.MESH)
+    own_weight = pltpu.make_async_copy(
+        weight, plane_weight.at[pl.ds(pl.multiple_of(spot * depth, depth), depth), :], own_sem.at[0]
+    )
+    own_context = pltpu.make_async_copy(
+        context.at[:, pl.ds(pl.multiple_of(line * span, span), span)],
+        line_context.at[token_rows(line), :],
+        own_sem.at[1],
+    )
+    own_weight.start()
+    own_context.start()
+    pl.semaphore_wait(barrier, near + far - 1)
+
+    for d in range(1, far):
+        context_copy(d).start()
+    for c in range(chunks):
+        for d in (3, 1, 2):
+            weight_copy(d, c).start()
+    own_weight.wait()
+    own_context.wait()
+    for d in range(1, far):
+        context_copy(d).wait_recv()
+        share_copy(d).start()
+    for d in range(1, far):
+        share_copy(d).wait_recv()
+
+    def multiply(c):
+        for d in range(1, near):
+            weight_copy(d, c).wait_recv()
+
+        def block(k, carry):
+            q = lax.select(line * 2 < far, far - 1 - k, k)
+            sums[token_rows(q), columns(c)] = jnp.dot(
+                line_context[token_rows(q), :], plane_weight[:, columns(c)], preferred_element_type=jnp.float32
+            )
+
+            @pl.when((line == 0) & (q > 0))
+            def _():
+                outgoing[token_rows(q), columns(c)] = sums[token_rows(q), columns(c)].astype(jnp.bfloat16)
+                right_copy(q, c).start()
+
+            @pl.when((line == far - 1) & (q < far - 1))
+            def _():
+                outgoing[token_rows(q), columns(c)] = sums[token_rows(q), columns(c)].astype(jnp.bfloat16)
+                left_copy(q, c).start()
+
+            return carry
+
+        lax.fori_loop(0, far, block, 0)
+
+    def pass_right(c):
+        def block(k, carry):
+            q = far - 1 - k
+            right_copy(q, c).wait_recv()
+            total = sums[token_rows(q), columns(c)] + from_left[token_rows(q), columns(c)].astype(jnp.float32)
+            outgoing[token_rows(q), columns(c)] = total.astype(jnp.bfloat16)
+            right_copy(q, c).start()
+            return carry
+
+        lax.fori_loop(0, lax.select(line > 0, far - 1 - line, 0), block, 0)
+
+    def pass_left(c):
+        def block(q, carry):
+            left_copy(q, c).wait_recv()
+            total = sums[token_rows(q), columns(c)] + from_right[token_rows(q), columns(c)].astype(jnp.float32)
+            outgoing[token_rows(q), columns(c)] = total.astype(jnp.bfloat16)
+            left_copy(q, c).start()
+            return carry
+
+        lax.fori_loop(0, lax.select(line < far - 1, line, 0), block, 0)
+
+    def forward(c):
+        @pl.when(line * 2 < far)
+        def _():
+            pass_right(c)
+            pass_left(c)
+
+        @pl.when(line * 2 >= far)
+        def _():
+            pass_left(c)
+            pass_right(c)
+
+    def step(c, carry):
+        multiply(c)
+
+        @pl.when(c > 0)
+        def _():
+            forward(c - 1)
+
+        return carry
+
+    lax.fori_loop(0, chunks, step, 0)
+    forward(chunks - 1)
+
+    def finish(c, carry):
+        sums[token_rows(line), columns(c)] += resid[:, columns(c)].astype(jnp.float32)
+
+        @pl.when(line > 0)
+        def _():
+            right_copy(line, c).wait_recv()
+            sums[token_rows(line), columns(c)] += from_left[token_rows(line), columns(c)].astype(jnp.float32)
+
+        @pl.when(line < far - 1)
+        def _():
+            left_copy(line, c).wait_recv()
+            sums[token_rows(line), columns(c)] += from_right[token_rows(line), columns(c)].astype(jnp.float32)
+
+        hidden[:, columns(c)] = sums[token_rows(line), columns(c)].astype(jnp.bfloat16)
+        return carry
+
+    lax.fori_loop(0, chunks, finish, 0)
+
+    for d in range(1, far):
+        context_copy(d).wait_send()
+        share_copy(d).wait_send()
+
+    def drain(c, carry):
+        for d in range(1, near):
+            weight_copy(d, c).wait_send()
+
+        def right_done(q, inner):
+            right_copy(q, c).wait_send()
+            return inner
+
+        def left_done(q, inner):
+            left_copy(q, c).wait_send()
+            return inner
+
+        lax.fori_loop(line + 1, far, right_done, 0)
+        lax.fori_loop(0, line, left_done, 0)
+        return carry
+
+    lax.fori_loop(0, chunks, drain, 0)
+
+
+def projected(resid, context, out_weight):
+    members = lax.axis_size("expert")
+    far = members // near
+    rows, half = resid.shape
+    depth = out_weight.shape[0]
+    dma = pltpu.SemaphoreType.DMA
+    return pl.pallas_call(
+        functools.partial(attention_kernel, members),
+        out_shape=jax.ShapeDtypeStruct((rows, half), jnp.bfloat16),
+        in_specs=[pl.BlockSpec(memory_space=pltpu.VMEM)] * 3,
+        out_specs=pl.BlockSpec(memory_space=pltpu.VMEM),
+        scratch_shapes=[
+            pltpu.VMEM((near * depth, half), jnp.bfloat16),
+            pltpu.VMEM((far * rows, near * depth), jnp.bfloat16),
+            pltpu.VMEM((far * rows, half), jnp.float32),
+            pltpu.VMEM((far * rows, half), jnp.bfloat16),
+            pltpu.VMEM((far * rows, half), jnp.bfloat16),
+            pltpu.VMEM((far * rows, half), jnp.bfloat16),
+            dma((2,)),
+            dma((near, chunks)),
+            dma((near, chunks)),
+            dma((far,)),
+            dma((far,)),
+            dma((far,)),
+            dma((far,)),
+            dma((far, chunks)),
+            dma((far, chunks)),
+            dma((far, chunks)),
+        ],
+        compiler_params=pltpu.CompilerParams(
+            collective_id=0, has_side_effects=True, vmem_limit_bytes=58 * 2**20
+        ),
+        name="projection",
+    )(resid, context, out_weight)
 
 
 def per_device(
@@ -20,30 +307,8 @@
 ):
     tok_rows, half_width = resid.shape
     members = lax.axis_size("expert")
-    near = 4
-    far = members // near
-    planes = [[p * near + i for i in range(near)] for p in range(far)]
-    lines = [[p * near + i for p in range(far)] for i in range(near)]
     pair_side = lax.axis_index("tensor")
-    k_rows = out_weight.shape[0]
-    plane_weight = lax.all_gather(out_weight, "expert", axis=0, tiled=True, axis_index_groups=planes)
-    context_parts = context.reshape(tok_rows, far, near * k_rows).transpose(1, 0, 2)
-    line_context = lax.all_to_all(
-        context_parts, "expert", split_axis=0, concat_axis=0, tiled=True, axis_index_groups=lines
-    )
-    partial = jnp.dot(
-        line_context.reshape(far * tok_rows, near * k_rows), plane_weight, preferred_element_type=jnp.float32
-    ).astype(jnp.bfloat16)
-    parts = lax.all_to_all(
-        partial.reshape(far, tok_rows, half_width),
-        "expert",
-        split_axis=0,
-        concat_axis=0,
-        tiled=True,
-        axis_index_groups=lines,
-    )
-    attention = jnp.sum(parts.astype(jnp.float32), axis=0)
-    hidden_state = (resid.astype(jnp.float32) + attention).astype(jnp.bfloat16)
+    hidden_state = projected(resid, context, out_weight)
     state_float = hidden_state.astype(jnp.float32)
     width = norm_gain.shape[0]
     squares = lax.psum(jnp.sum(state_float * state_float, axis=1, keepdims=True), "tensor")

time: 277 us -> 217 us (0.78)
  the two profiles are of different devices: /device:TPU:7 before, /device:TPU:12 now
where the time goes in v2:
time: 217 us
  Pallas kernels  80.3 us (37%)
  blocking collectives  47.7 us (22%)
  waiting for transfers between devices  47.6 us (22%)
  matrix products  15.9 us (7%)
  between operations  13.5 us (6%)
  starting transfers between devices  7.09 us (3%)
  other arithmetic  3.89 us (2%)
    pallas_call x1, Pallas kernels, projected(): pl.pallas_call(functools.partial(attention_kernel, members), out_shape=ja...  80.3 us
    all_to_all x1, blocking collectives, per_device(): lax.all_to_all(packed, 'expert', split_axis=0, concat_axis=0, tiled=True)  43 us
    all_to_all x1, waiting for transfers between devices, per_device(): lax.all_to_all(product, 'expert', split_axis=0, concat_axis=0, tiled=True)  36 us
    all_gather x1, waiting for transfers between devices, per_device(): flat_rows = lax.all_gather(flat_rows, 'tensor', axis=1, tiled=True)  11.6 us
    all_to_all x1, starting transfers between devices, per_device(): lax.all_to_all(product, 'expert', split_axis=0, concat_axis=0, tiled=True)  7.08 us
    dot_general x1, matrix products, per_device(): jnp.dot(flat_rows, gate_up[0, 0], preferred_element_type=jnp.float32)  4.76 us
  transfers between devices with their start and end apart: 2, of which 2 were waited for; matrix products, arithmetic and copies ran while one was open for 1% of the time, Pallas kernels for 0%

profile of v2, /device:TPU:12, one launch (start us, length us, event | category | flops | bytes accessed | tf_op | source)
XLA Modules:
  0.0 217.0 jit_solution(6880247179965312830)
XLA Ops:
  6.5 0.0 copy-start
  6.5 0.0 copy-start.5
  6.5 0.0 all-gather.2.cloned.1.call-start
  6.5 0.9 eq.167
  7.5 80.3 %projection.1 = bf16[192,2048]{1,0:T(8,128)(2,1)} custom-call(bf16[192,2048]{1,0:T(8,128)(2,1)} %resid.1, bf16[192,4096]{1,0:T(8,128)(2,1)} %context.1, bf16[256,2048]{1,0:T(8,128)(2,1)} %weight.1), custom_call_target="tpu_custom_call" | custom-call | tf_op jit(solution)/shard_map/projection/pallas_call | solution.py:266
  87.8 1.4 fusion.11
  89.1 2.5 %psum.7 = f32[192,1]{0,1:T(1,128)S(1)} all-reduce(f32[192,1]{0,1:T(1,128)S(1)} %bitcast.66), channel_id=1, replica_groups=mesh['group'=1,'expert'=16,'tensor'=2] {'tensor'}, use_global_device_ids=true, to_apply=%region_1.0 | all-reduce | flops 192 | bytes 1536 | tf_op jit(solution)/shard_map/psum | solution.py:314
  91.6 0.0 copy-done.5
  91.6 1.8 convolution_convert_fusion
  93.5 43.0 %all_to_all.10 = bf16[16,24,2048]{2,1,0:T(8,128)(2,1)} all-to-all(bf16[16,24,2048]{2,1,0:T(8,128)(2,1)S(1)} %bitcast.46), channel_id=1, replica_groups=mesh['group'=1,'expert'=16,'tensor'=2] {'expert'}, dimensions={0} | all-to-all | bytes 3145728 | tf_op jit(solution)/shard_map/all_to_all | solution.py:323
  136.5 0.0 all-gather.2.cloned.1.call-update
  136.5 11.6 %all-gather.2.cloned.1.call-done = bf16[384,4096]{1,0:T(8,128)(2,1)} async-done(((bf16[384,2048]{1,0:T(8,128)(2,1)}), bf16[384,4096]{1,0:T(8,128)(2,1)}) %all-gather.2.cloned.1.call-update) | async-done | bytes 3145744 | tf_op jit(solution)/shard_map/all_gather | solution.py:325
  148.1 0.0 copy-start.6
  148.1 4.8 %fusion.4 = f32[384,384]{1,0:T(8,128)S(1)} fusion(bf16[384,4096]{1,0:T(8,128)(2,1)} %all-gather.2.cloned.1.call-done, bf16[1,2,4096,384]{3,2,1,0:T(8,128)(2,1)} %param.14), kind=kOutput, calls=%fused_computation.4 | convolution fusion | flops 1207959552 | bytes 6881280 | tf_op jit(solution)/shard_map/dot_general | solution.py:326
  152.9 0.0 copy-done.6
  152.9 3.7 %fusion.18 = bf16[384,384]{1,0:T(8,128)(2,1)S(1)} fusion(bf16[384,4096]{1,0:T(8,128)(2,1)S(1)} %copy-done.6, bf16[1,2,4096,384]{3,2,1,0:T(8,128)(2,1)} %param.14, f32[384,384]{1,0:T(8,128)S(1)} %fusion.4), kind=kOutput, calls=%fused_computation.19 | convolution fusion | flops 1208844288 | bytes 7176192 | tf_op jit(solution)/shard_map/dot_general | solution.py:327
  156.6 2.2 %all_gather.7 = bf16[384,768]{1,0:T(8,128)(2,1)S(1)} all-gather(bf16[384,384]{1,0:T(8,128)(2,1)S(1)} %fusion.18), channel_id=1, replica_groups=mesh['group'=1,'expert'=16,'tensor'=2] {'tensor'}, dimensions={1}, use_global_device_ids=true | all-gather | bytes 884736 | tf_op jit(solution)/shard_map/all_gather | solution.py:329
  158.8 0.0 copy-done
  158.8 2.6 %fusion.8 = bf16[384,2048]{1,0:T(8,128)(2,1)} fusion(bf16[384,768]{1,0:T(8,128)(2,1)S(1)} %all_gather.7, bf16[1,768,2048]{2,1,0:T(8,128)(2,1)S(1)} %copy-done), kind=kOutput, calls=%fused_computation.8 | convolution fusion | flops 1208745984 | bytes 5308416 | tf_op jit(solution)/shard_map/dot_general | solution.py:330
  161.4 0.0 copy-start.2
  161.4 0.0 copy-start.3
  161.4 0.0 copy-start.4
  161.4 7.1 %all-to-all-start.1 = ((bf16[16,24,2048]{2,1,0:T(8,128)(2,1)}), bf16[16,24,2048]{2,1,0:T(8,128)(2,1)}, u32[]{:S(2)}, u32[]{:S(2)}) async-start(bf16[16,24,2048]{2,1,0:T(8,128)(2,1)} %bitcast.47), calls=%async_computation.1 | async-start | bytes 3145728 | tf_op jit(solution)/shard_map/all_to_all | solution.py:332
  168.5 0.0 copy-done.2
  168.5 0.0 copy-done.3
  168.5 0.0 copy-done.4
  168.5 0.6 reduce-precision_convert_fusion.1
  169.2 0.8 pad_maximum_fusion
  170.0 36.0 %all-to-all-done.1 = bf16[16,24,2048]{2,1,0:T(8,128)(2,1)} async-done(((bf16[16,24,2048]{2,1,0:T(8,128)(2,1)}), bf16[16,24,2048]{2,1,0:T(8,128)(2,1)}, u32[]{:S(2)}, u32[]{:S(2)}) %all-to-all-start.1) | async-done | bytes 1572896 | tf_op jit(solution)/shard_map/all_to_all | solution.py:332
  206.0 3.1 %convolution_reduce_fusion = f32[192,2048]{1,0:T(8,128)S(1)} fusion(bf16[3,192,384]{2,1,0:T(8,128)(2,1)} %bitcast.48, bf16[384,2048,1]{1,0,2:T(8,128)(2,1)} %bitcast.26), kind=kOutput, calls=%fused_computation.13 | convolution fusion | flops 906756096 | bytes 3588096 | tf_op jit(solution)/shard_map/dot_general | solution.py:343
  209.1 0.0 copy-done.1
  209.1 1.1 fusion.14
  (6 shorter events, 0.0 us)
Async XLA Ops:
  6.5 152.3 %copy-start = (bf16[1,768,2048]{2,1,0:T(8,128)(2,1)S(1)}, bf16[1,768,2048]{2,1,0:T(8,128)(2,1)}, u32[]{:S(2)}) copy-start(bf16[1,768,2048]{2,1,0:T(8,128)(2,1)} %param.15) | copy-start | bytes 9437188
  6.5 85.1 %copy-start.5 = (f32[4096]{0:T(1024)S(1)}, f32[4096]{0:T(1024)}, u32[]{:S(2)}) copy-start(f32[4096]{0:T(1024)} %param.13) | copy-start | bytes 49156
  6.5 141.5 %all-gather.2.cloned.1.call-start = ((), (), s32[]{:S(2)}) async-start(), calls=%async_computation.2 | async-start | bytes 4718592 | tf_op jit(solution)/shard_map/all_gather | solution.py:325
  148.1 4.8 %copy-start.6 = (bf16[384,4096]{1,0:T(8,128)(2,1)S(1)}, bf16[384,4096]{1,0:T(8,128)(2,1)}, u32[]{:S(2)}) copy-start(bf16[384,4096]{1,0:T(8,128)(2,1)} %all-gather.2.cloned.1.call-done) | copy-start | bytes 9437188
  161.4 7.1 %copy-start.2 = (s32[192,8]{0,1:T(8,128)S(1)}, s32[192,8]{0,1:T(8,128)}, u32[]{:S(2)}) copy-start(s32[192,8]{0,1:T(8,128)} %param.17) | copy-start | bytes 18436
  161.4 7.1 %copy-start.3 = (s32[192,8]{0,1:T(8,128)S(1)}, s32[192,8]{0,1:T(8,128)}, u32[]{:S(2)}) copy-start(s32[192,8]{0,1:T(8,128)} %param.16) | copy-start | bytes 18436
  161.4 7.1 %copy-start.4 = (f32[192,8]{0,1:T(8,128)S(1)}, f32[192,8]{0,1:T(8,128)}, u32[]{:S(2)}) copy-start(f32[192,8]{0,1:T(8,128)} %param.19) | copy-start | bytes 18436
  161.4 44.6 %all-to-all-start.1 = ((bf16[16,24,2048]{2,1,0:T(8,128)(2,1)}), bf16[16,24,2048]{2,1,0:T(8,128)(2,1)}, u32[]{:S(2)}, u32[]{:S(2)}) async-start(bf16[16,24,2048]{2,1,0:T(8,128)(2,1)} %bitcast.47), calls=%async_computation.1 | async-start | bytes 3145728 | tf_op jit(solution)/shard_map/all_to_all | solution.py:332
  206.0 3.1 %copy-start.1 = (bf16[192,2048]{1,0:T(8,128)(2,1)S(1)}, bf16[192,2048]{1,0:T(8,128)(2,1)}, u32[]{:S(2)}) copy-start(bf16[192,2048]{1,0:T(8,128)(2,1)} %projection.1) | copy-start | bytes 2359300
Sparse Core Ops, SparseCore 0:
  136.6 11.4 all-gather.1

commit v3 on v2

v3 whole, which is shorter than its diff:
```python
import functools

import jax
import jax.numpy as jnp
from jax import lax
from jax.experimental import pallas as pl
from jax.experimental.pallas import tpu as pltpu
from jax.sharding import PartitionSpec as P

epsilon = 1e-06
near = 4
chunks = 4


def layer_kernel(
    members,
    resid,
    context,
    weight,
    gain,
    pick,
    gate_up,
    down_weight,
    hidden,
    returned,
    plane_weight,
    line_context,
    sums,
    travel,
    squares,
    stacked,
    packed,
    features,
    gate_up_local,
    down_local,
    active,
    product,
    own_sem,
    weight_send,
    weight_recv,
    context_send,
    context_recv,
    share_send,
    share_recv,
    chain_send,
    left_recv,
    right_recv,
    square_send,
    square_recv,
    row_send,
    row_recv,
    pair_send,
    pair_recv,
    active_send,
    active_recv,
    back_send,
    back_recv,
):
    far = members // near
    me = lax.axis_index("expert")
    side = lax.axis_index("tensor")
    line = lax.div(me, near)
    spot = lax.rem(me, near)
    rows, half = resid.shape
    depth = weight.shape[0]
    span = near * depth
    piece = span // 2
    wide = half // chunks

    def columns(c):
        return pl.ds(pl.multiple_of(c * wide, wide), wide)

    def token_rows(q):
        return pl.ds(pl.multiple_of(q * rows, rows), rows)

    own_columns = pl.ds(pl.multiple_of(side * piece, piece), piece)

    def weight_copy(d, c):
        slot = pl.ds(pl.multiple_of(spot * depth, depth), depth)
        return pltpu.make_async_remote_copy(
            src_ref=weight.at[:, columns(c)],
            dst_ref=plane_weight.at[slot, columns(c)],
            send_sem=weight_send.at[d, c],
            recv_sem=weight_recv.at[d, c],
            device_id={"expert": line * near + lax.bitwise_xor(spot, d)},
            device_id_type=pl.DeviceIdType.MESH,
        )

    def context_copy(d):
        target = lax.rem(line + d, far)
        return pltpu.make_async_remote_copy(
            src_ref=context.at[:, pl.ds(pl.multiple_of(target * span + side * piece, piece), piece)],
            dst_ref=line_context.at[token_rows(line), own_columns],
            send_sem=context_send.at[d],
            recv_sem=context_recv.at[d],
            device_id={"expert": target * near + spot},
            device_id_type=pl.DeviceIdType.MESH,
        )

    def share_copy(d):
        place = line_context.at[token_rows(lax.rem(line - d + far, far)), own_columns]
        return pltpu.make_async_remote_copy(
            src_ref=place,
            dst_ref=place,
            send_sem=share_send.at[d],
            recv_sem=share_recv.at[d],
            device_id={"tensor": 1 - side},
            device_id_type=pl.DeviceIdType.MESH,
        )

    def right_copy(q, c):
        return pltpu.make_async_remote_copy(
            src_ref=travel.at[token_rows(q), columns(c)],
            dst_ref=travel.at[token_rows(q), columns(c)],
            send_sem=chain_send.at[q, c],
            recv_sem=left_recv.at[q, c],
            device_id={"expert": me + near},
            device_id_type=pl.DeviceIdType.MESH,
        )

    def left_copy(q, c):
        return pltpu.make_async_remote_copy(
            src_ref=travel.at[token_rows(q), columns(c)],
            dst_ref=travel.at[token_rows(lax.select(q == line - 1, far, q)), columns(c)],
            send_sem=chain_send.at[q, c],
            recv_sem=right_recv.at[q, c],
            device_id={"expert": me - near},
            device_id_type=pl.DeviceIdType.MESH,
        )

    barrier = pltpu.get_barrier_semaphore()
    def greet(d, carry):
        pl.semaphore_signal(
            barrier,
            inc=1,
            device_id={"expert": lax.rem(me + d, members)},
            device_id_type=pl.DeviceIdType.MESH,
        )
        return carry

    lax.fori_loop(1, members, greet, 0)
    pl.semaphore_signal(barrier, inc=1, device_id={"tensor": 1 - side}, device_id_type=pl.DeviceIdType.MESH)
    own_weight = pltpu.make_async_copy(
        weight, plane_weight.at[pl.ds(pl.multiple_of(spot * depth, depth), depth), :], own_sem.at[0]
    )
    own_context = pltpu.make_async_copy(
        context.at[:, pl.ds(pl.multiple_of(line * span, span), span)],
        line_context.at[token_rows(line), :],
        own_sem.at[1],
    )
    own_weight.start()
    own_context.start()
    pl.semaphore_wait(barrier, members)

    for d in range(1, far):
        context_copy(d).start()
    for c in range(chunks):
        for d in (3, 1, 2):
            weight_copy(d, c).start()
    ffe = gate_up.shape[3]
    loads = [
        pltpu.make_async_copy(gate_up.at[0, 0], gate_up_local.at[:, :ffe], own_sem.at[2]),
        pltpu.make_async_copy(gate_up.at[0, 1], gate_up_local.at[:, ffe:], own_sem.at[3]),
        pltpu.make_async_copy(down_weight.at[0], down_local, own_sem.at[4]),
    ]
    for load in loads:
        load.start()
    own_weight.wait()
    own_context.wait()
    for d in range(1, far):
        context_copy(d).wait_recv()
        share_copy(d).start()
    for d in range(1, far):
        share_copy(d).wait_recv()

    def multiply(c):
        for d in range(1, near):
            weight_copy(d, c).wait_recv()

        def block(k, carry):
            q = lax.select(line * 2 < far, far - 1 - k, k)
            sums[token_rows(q), columns(c)] = jnp.dot(
                line_context[token_rows(q), :], plane_weight[:, columns(c)], preferred_element_type=jnp.float32
            )

            @pl.when((line == 0) & (q > 0))
            def _():
                travel[token_rows(q), columns(c)] = sums[token_rows(q), columns(c)].astype(jnp.bfloat16)
                right_copy(q, c).start()

            @pl.when((line == far - 1) & (q < far - 1))
            def _():
                travel[token_rows(q), columns(c)] = sums[token_rows(q), columns(c)].astype(jnp.bfloat16)
                left_copy(q, c).start()

            return carry

        lax.fori_loop(0, far, block, 0)

    def pass_right(c):
        def block(k, carry):
            q = far - 1 - k
            right_copy(q, c).wait_recv()
            total = sums[token_rows(q), columns(c)] + travel[token_rows(q), columns(c)].astype(jnp.float32)
            travel[token_rows(q), columns(c)] = total.astype(jnp.bfloat16)
            right_copy(q, c).start()
            return carry

        lax.fori_loop(0, lax.select(line > 0, far - 1 - line, 0), block, 0)

    def pass_left(c):
        def block(q, carry):
            left_copy(q, c).wait_recv()
            total = sums[token_rows(q), columns(c)] + travel[token_rows(q), columns(c)].astype(jnp.float32)
            travel[token_rows(q), columns(c)] = total.astype(jnp.bfloat16)
            left_copy(q, c).start()
            return carry

        lax.fori_loop(0, lax.select(line < far - 1, line, 0), block, 0)

    def forward(c):
        @pl.when(line * 2 < far)
        def _():
            pass_right(c)
            pass_left(c)

        @pl.when(line * 2 >= far)
        def _():
            pass_left(c)
            pass_right(c)

    def step(c, carry):
        multiply(c)

        @pl.when(c > 0)
        def _():
            forward(c - 1)

        return carry

    lax.fori_loop(0, chunks, step, 0)
    forward(chunks - 1)

    def finish(c, carry):
        sums[token_rows(line), columns(c)] += resid[:, columns(c)].astype(jnp.float32)

        @pl.when(line > 0)
        def _():
            right_copy(line, c).wait_recv()
            sums[token_rows(line), columns(c)] += travel[token_rows(line), columns(c)].astype(jnp.float32)

        @pl.when(line < far - 1)
        def _():
            left_copy(line, c).wait_recv()
            sums[token_rows(line), columns(c)] += travel[token_rows(far), columns(c)].astype(jnp.float32)

        state = sums[token_rows(line), columns(c)].astype(jnp.bfloat16)
        hidden[:, columns(c)] = state
        state_float = state.astype(jnp.float32)
        square = state_float * state_float
        squares[0] += sum(square[:, k * 128 : (k + 1) * 128] for k in range(wide // 128))
        return carry

    squares[0] = jnp.zeros((rows, 128), jnp.float32)
    lax.fori_loop(0, chunks, finish, 0)

    square_copy = pltpu.make_async_remote_copy(
        src_ref=squares.at[0],
        dst_ref=squares.at[1],
        send_sem=square_send,
        recv_sem=square_recv,
        device_id={"tensor": 1 - side},
        device_id_type=pl.DeviceIdType.MESH,
    )
    square_copy.start()
    square_copy.wait()
    mean = jnp.sum(squares[0] + squares[1], axis=1, keepdims=True) / (2 * half)
    row_scale = lax.rsqrt(mean + epsilon)
    quarter = half // 2
    for c in range(chunks):
        at, of = c // (chunks // 2), c % (chunks // 2)
        here = slice(c * wide, (c + 1) * wide)
        normed = hidden[:, here].astype(jnp.float32) * row_scale * gain[pl.ds(side, 1), here]
        stacked[at * rows : (at + 1) * rows, of * wide : (of + 1) * wide] = normed.astype(jnp.bfloat16)

    both = pick.shape[0] // members
    cap = both // 2

    def slot_rows(e):
        return pl.ds(pl.multiple_of(e * both, both), both)

    def plane_rows(q, size):
        return pl.ds(pl.multiple_of(q * near * size, near * size), near * size)

    own_features = pltpu.make_async_copy(packed.at[slot_rows(me), :], features.at[side, slot_rows(me), :], own_sem.at[5])
    own_product = pltpu.make_async_copy(product.at[slot_rows(me), :], returned.at[slot_rows(me), :], own_sem.at[6])

    def row_copy(target, source):
        return pltpu.make_async_remote_copy(
            src_ref=packed.at[slot_rows(target), :],
            dst_ref=features.at[side, slot_rows(source), :],
            send_sem=row_send.at[target],
            recv_sem=row_recv.at[source],
            device_id={"expert": target},
            device_id_type=pl.DeviceIdType.MESH,
        )

    def pair_copy(q):
        place = features.at[side, plane_rows(q, both), :]
        return pltpu.make_async_remote_copy(
            src_ref=place,
            dst_ref=place,
            send_sem=pair_send.at[q],
            recv_sem=pair_recv.at[q],
            device_id={"tensor": 1 - side},
            device_id_type=pl.DeviceIdType.MESH,
        )

    def active_copy(q):
        place = active.at[plane_rows(q, cap), pl.ds(pl.multiple_of(side * ffe, ffe), ffe)]
        return pltpu.make_async_remote_copy(
            src_ref=place,
            dst_ref=place,
            send_sem=active_send.at[q],
            recv_sem=active_recv.at[q],
            device_id={"tensor": 1 - side},
            device_id_type=pl.DeviceIdType.MESH,
        )

    def back_copy(target, source):
        return pltpu.make_async_remote_copy(
            src_ref=product.at[slot_rows(target), :],
            dst_ref=returned.at[slot_rows(source), :],
            send_sem=back_send.at[target],
            recv_sem=back_recv.at[source],
            device_id={"expert": target},
            device_id_type=pl.DeviceIdType.MESH,
        )

    def near_first(k):
        return lax.select(line * 2 < far, k, far - 1 - k)

    def dispatch(k, carry):
        q = near_first(far - 1 - k)
        packed[plane_rows(q, both), :] = jnp.dot(
            pick[plane_rows(q, both), :], stacked[...], preferred_element_type=jnp.float32
        ).astype(jnp.bfloat16)
        for j in range(near):
            target = q * near + j

            @pl.when(target != me)
            def _():
                row_copy(target, me).start()

            @pl.when(target == me)
            def _():
                own_features.start()

        return carry

    lax.fori_loop(0, far, dispatch, 0)
    for load in loads:
        load.wait()

    def expert_step(k, carry):
        @pl.when(k < far)
        def _():
            q = near_first(k)
            for j in range(near):
                source = q * near + j

                @pl.when(source != me)
                def _():
                    row_copy(source, source).wait_recv()

                @pl.when(source == me)
                def _():
                    own_features.wait()

            pair_copy(q).start()

        @pl.when((k >= 1) & (k < far + 1))
        def _():
            q = near_first(k - 1)
            pair_copy(q).wait_recv()
            parts = []
            for h in range(2):
                total = None
                for t in range(2):
                    first = t * half + h * quarter
                    term = jnp.dot(
                        features[t, plane_rows(q, both), :],
                        gate_up_local[first : first + quarter, :],
                        preferred_element_type=jnp.float32,
                    )
                    total = term if total is None else total + term
                parts.append(total)
            joined = jnp.concatenate(
                [
                    parts[0][j * both : j * both + cap] + parts[1][j * both + cap : (j + 1) * both]
                    for j in range(near)
                ],
                axis=0,
            )
            gate, up = joined[:, :ffe], joined[:, ffe:]
            active[plane_rows(q, cap), pl.ds(pl.multiple_of(side * ffe, ffe), ffe)] = (
                gate / (1.0 + jnp.exp(-gate)) * up
            ).astype(jnp.bfloat16)
            active_copy(q).start()

        @pl.when(k >= 2)
        def _():
            q = near_first(k - 2)
            active_copy(q).wait()
            out = jnp.dot(active[plane_rows(q, cap), :], down_local[...], preferred_element_type=jnp.float32)
            for j in range(near):
                target = q * near + j
                mine = out[j * cap : (j + 1) * cap]
                product[slot_rows(target), :] = jnp.concatenate(
                    [mine[:, :quarter], mine[:, quarter:]], axis=0
                ).astype(jnp.bfloat16)

                @pl.when(target != me)
                def _():
                    back_copy(target, me).start()

                @pl.when(target == me)
                def _():
                    own_product.start()

        return carry

    lax.fori_loop(0, far + 2, expert_step, 0)
    own_product.wait()

    def settle(d, carry):
        other = lax.rem(me + d, members)
        back_copy(other, other).wait_recv()
        back_copy(other, me).wait_send()
        row_copy(other, me).wait_send()
        return carry

    lax.fori_loop(1, members, settle, 0)
    for q in range(far):
        pair_copy(q).wait_send()

    for d in range(1, far):
        context_copy(d).wait_send()
        share_copy(d).wait_send()

    def drain(c, carry):
        for d in range(1, near):
            weight_copy(d, c).wait_send()

        def right_done(q, inner):
            right_copy(q, c).wait_send()
            return inner

        def left_done(q, inner):
            left_copy(q, c).wait_send()
            return inner

        lax.fori_loop(line + 1, far, right_done, 0)
        lax.fori_loop(0, line, left_done, 0)
        return carry

    lax.fori_loop(0, chunks, drain, 0)


def layer(resid, context, out_weight, gain, pick, gate_up, down_weight):
    members = lax.axis_size("expert")
    far = members // near
    rows, half = resid.shape
    depth = out_weight.shape[0]
    slot_rows = pick.shape[0]
    width, ffe = gate_up.shape[2:]
    dma = pltpu.SemaphoreType.DMA
    vmem = pl.BlockSpec(memory_space=pltpu.VMEM)
    far_spec = pl.BlockSpec(memory_space=pl.ANY)
    wire = jnp.bfloat16
    return pl.pallas_call(
        functools.partial(layer_kernel, members),
        out_shape=[
            jax.ShapeDtypeStruct((rows, half), wire),
            jax.ShapeDtypeStruct((slot_rows, half // 2), wire),
        ],
        in_specs=[vmem] * 5 + [far_spec] * 2,
        out_specs=[vmem, vmem],
        scratch_shapes=[
            pltpu.VMEM((near * depth, half), wire),
            pltpu.VMEM((far * rows, near * depth), wire),
            pltpu.VMEM((far * rows, half), jnp.float32),
            pltpu.VMEM(((far + 1) * rows, half), wire),
            pltpu.VMEM((2, rows, 128), jnp.float32),
            pltpu.VMEM((2 * rows, half // 2), wire),
            pltpu.VMEM((slot_rows, half // 2), wire),
            pltpu.VMEM((2, slot_rows, half // 2), wire),
            pltpu.VMEM((width, 2 * ffe), wire),
            pltpu.VMEM((2 * ffe, half), wire),
            pltpu.VMEM((slot_rows // 2, 2 * ffe), wire),
            pltpu.VMEM((slot_rows, half // 2), wire),
            dma((7,)),
            dma((near, chunks)),
            dma((near, chunks)),
            dma((far,)),
            dma((far,)),
            dma((far,)),
            dma((far,)),
            dma((far, chunks)),
            dma((far, chunks)),
            dma((far, chunks)),
            dma,
            dma,
            dma((members,)),
            dma((members,)),
            dma((far,)),
            dma((far,)),
            dma((far,)),
            dma((far,)),
            dma((members,)),
            dma((members,)),
        ],
        compiler_params=pltpu.CompilerParams(
            collective_id=0, has_side_effects=True, vmem_limit_bytes=60 * 2**20
        ),
        name="layer",
    )(resid, context, out_weight, gain, pick, gate_up, down_weight)


def per_device(
    resid,
    context,
    out_weight,
    norm_gain,
    gate_up,
    down_weight,
    expert_ids,
    slots,
    token_order,
    combine,
):
    tok_rows, half_width = resid.shape
    members, capacity = token_order.shape
    halves = jnp.arange(2, dtype=jnp.int32)
    tokens = jnp.arange(tok_rows, dtype=jnp.int32)
    pick = (token_order[:, None, :, None, None] == tokens) & (
        halves[None, :, None, None, None] == halves[None, None, None, :, None]
    )
    pick = pick.astype(jnp.bfloat16).reshape(members * 2 * capacity, 2 * tok_rows)
    hidden_state, table = layer(
        resid, context, out_weight, norm_gain.reshape(2, half_width), pick, gate_up, down_weight
    )
    flat_index = jnp.where(slots >= 0, (expert_ids * 2) * capacity + slots, -1)
    places = jnp.arange(members * 2 * capacity, dtype=jnp.int32)
    sums = []
    for h in range(2):
        weights = jnp.zeros((tok_rows, members * 2 * capacity), jnp.float32)
        for column in range(expert_ids.shape[1]):
            match = (flat_index[:, column, None] + h * capacity == places[None, :]) & (slots[:, column, None] >= 0)
            weights = weights + jnp.where(match, combine[:, column, None], 0.0)
        high = lax.reduce_precision(weights, 8, 7)
        low = lax.reduce_precision(weights - high, 8, 7)
        two = jnp.concatenate([high, low], axis=0).astype(jnp.bfloat16)
        total = jnp.dot(two, table, preferred_element_type=jnp.float32)
        sums.append(total[:tok_rows] + total[tok_rows:])
    mixed_sum = jnp.concatenate(sums, axis=1)
    return (hidden_state.astype(jnp.float32) + mixed_sum).astype(jnp.bfloat16)


def solution(mesh):
    placed = (
        P(("group", "expert"), "tensor"),
        P(("group", "expert"), None),
        P("expert", "tensor"),
        P(),
        P("expert", None, None, "tensor"),
        P("expert", None, "tensor"),
        P(("group", "expert"), None),
        P(("group", "expert"), None),
        P(("group", "expert"), None),
        P(("group", "expert"), None),
    )
    return jax.shard_map(
        per_device,
        mesh=mesh,
        in_specs=placed,
        out_specs=P(("group", "expert"), "tensor"),
        check_vma=False,
    )
```

time: 217 us -> 184 us (0.85)
  the two profiles are of different devices: /device:TPU:12 before, /device:TPU:7 now
where the time goes in v3:
time: 184 us
  Pallas kernels  166 us (90%)
  other arithmetic  10.4 us (6%)
  local copies, waits for them, and re-layouts  4.32 us (2%)
  matrix products  3.07 us (2%)
    pallas_call x1, Pallas kernels, layer(): pl.pallas_call(functools.partial(layer_kernel, members), out_shape=[jax.S...  166 us
    another operation x4, other arithmetic  5.46 us

profile of v3, /device:TPU:7, one launch (start us, length us, event | category | flops | bytes accessed | tf_op | source)
XLA Modules:
  0.0 183.7 jit_solution(12505624038996331254)
XLA Ops:
  0.0 1.0 compare_reduce_fusion.7
  1.0 0.7 add_select_fusion
  1.8 1.0 fusion.32
  2.8 1.3 reshape.33.gain
  4.1 0.8 iota_compare_fusion.16
  4.9 1.4 fusion.4
  6.4 1.3 reduce-precision_convert_fusion
  7.7 1.4 fusion.2
  9.1 1.3 reduce-precision_convert_fusion.1
  10.4 1.0 and_convert_fusion
  11.4 1.2 reshape.34.pick
  12.6 165.8 %layer.1 = (bf16[192,2048]{1,0:T(8,128)(2,1)}, bf16[768,1024]{1,0:T(8,128)(2,1)}) custom-call(bf16[192,2048]{1,0:T(8,128)(2,1)} %resid.1, bf16[192,4096]{1,0:T(8,128)(2,1)} %context.1, bf16[256,2048]{1,0:T(8,128)(2,1)} %weight.1, f32[2,2048]{1,0:T(2,128)} %reshape.33.gain, bf16[768,384]{1,0:T(8,128)(2,1)} %reshape.34.pick, ...), custom_call_target="tpu_custom_call" | custom-call | tf_op jit(solution)/shard_map/layer/pallas_call | solution.py:481
  178.4 0.0 copy-start
  178.4 2.3 %fusion.9 = f32[384,1024]{1,0:T(8,128)S(1)} fusion(bf16[768,1024]{1,0:T(8,128)(2,1)} %get-tuple-element.8, bf16[192,768]{1,0:T(8,128)(2,1)S(1)} %fusion.4, bf16[192,768]{1,0:T(8,128)(2,1)S(1)} %reduce-precision_convert_fusion), kind=kOutput, calls=%fused_computation.17 | convolution fusion | flops 605159424 | bytes 3735552 | tf_op jit(solution)/shard_map/dot_general | solution.py:564
  180.7 0.0 copy-done
  180.7 0.8 fusion.5
  181.5 0.0 copy-start.1
  181.5 0.4 slice_add_fusion
  181.9 0.8 copy-done.1
  182.7 1.1 fusion
  (2 shorter events, 0.0 us)
Async XLA Ops:
  178.4 2.3 %copy-start = (bf16[768,1024]{1,0:T(8,128)(2,1)S(1)}, bf16[768,1024]{1,0:T(8,128)(2,1)}, u32[]{:S(2)}) copy-start(bf16[768,1024]{1,0:T(8,128)(2,1)} %get-tuple-element.8) | copy-start | bytes 4718596
  181.5 1.1 copy-start.1

commit v4 on v3

--- a/solution.py
+++ b/solution.py
@@ -9,7 +9,7 @@
 
 epsilon = 1e-06
 near = 4
-chunks = 4
+chunks = 8
 
 
 def layer_kernel(
@@ -18,11 +18,13 @@
     context,
     weight,
     gain,
-    pick,
+    order,
+    expert_ids,
+    slots,
+    combine,
     gate_up,
     down_weight,
-    hidden,
-    returned,
+    mixed,
     plane_weight,
     line_context,
     sums,
@@ -35,6 +37,10 @@
     down_local,
     active,
     product,
+    hidden,
+    returned,
+    pick,
+    weights,
     own_sem,
     weight_send,
     weight_recv,
@@ -165,13 +171,13 @@
     ]
     for load in loads:
         load.start()
+    wanted = order[...]
+    pick[...] = jnp.where(wanted == lax.broadcasted_iota(jnp.int32, pick.shape, 1), 1.0, 0.0).astype(jnp.bfloat16)
     own_weight.wait()
     own_context.wait()
     for d in range(1, far):
         context_copy(d).wait_recv()
         share_copy(d).start()
-    for d in range(1, far):
-        share_copy(d).wait_recv()
 
     def multiply(c):
         for d in range(1, near):
@@ -179,6 +185,11 @@
 
         def block(k, carry):
             q = lax.select(line * 2 < far, far - 1 - k, k)
+
+            @pl.when((c == 0) & (q != line))
+            def _():
+                share_copy(lax.rem(line - q + far, far)).wait_recv()
+
             sums[token_rows(q), columns(c)] = jnp.dot(
                 line_context[token_rows(q), :], plane_weight[:, columns(c)], preferred_element_type=jnp.float32
             )
@@ -280,7 +291,7 @@
     for c in range(chunks):
         at, of = c // (chunks // 2), c % (chunks // 2)
         here = slice(c * wide, (c + 1) * wide)
-        normed = hidden[:, here].astype(jnp.float32) * row_scale * gain[pl.ds(side, 1), here]
+        normed = hidden[:, here].astype(jnp.float32) * row_scale * gain[:, pl.ds(pl.multiple_of(side * half + c * wide, wide), wide)]
         stacked[at * rows : (at + 1) * rows, of * wide : (of + 1) * wide] = normed.astype(jnp.bfloat16)
 
     both = pick.shape[0] // members
@@ -359,6 +370,23 @@
         return carry
 
     lax.fori_loop(0, far, dispatch, 0)
+    def weigh(q, carry):
+        flat = expert_ids[...] * both + slots[...] - q * near * both
+        live = slots[...] >= 0
+        share = jnp.where(live, combine[...], 0.0)
+        for h in range(2):
+            place = lax.broadcasted_iota(jnp.int32, (rows, near * both), 1) - h * cap
+            total = jnp.zeros((rows, near * both), jnp.float32)
+            for k in range(expert_ids.shape[1]):
+                same = live[:, k : k + 1] & (flat[:, k : k + 1] == place)
+                total = total + jnp.where(same, share[:, k : k + 1], 0.0)
+            high = total.astype(jnp.bfloat16)
+            weights[q, h, :rows, :] = high
+            weights[q, h, rows:, :] = (total - high.astype(jnp.float32)).astype(jnp.bfloat16)
+        return carry
+
+    lax.fori_loop(0, far, weigh, 0)
+    sums[:rows, :] = hidden[...].astype(jnp.float32)
     for load in loads:
         load.wait()
 
@@ -431,11 +459,32 @@
         return carry
 
     lax.fori_loop(0, far + 2, expert_step, 0)
-    own_product.wait()
+
+    def mix(k, carry):
+        q = near_first(k)
+        for j in range(near):
+            source = q * near + j
+
+            @pl.when(source != me)
+            def _():
+                back_copy(source, source).wait_recv()
+
+            @pl.when(source == me)
+            def _():
+                own_product.wait()
+
+        for h in range(2):
+            both_parts = jnp.dot(
+                weights[q, h], returned[plane_rows(q, both), :], preferred_element_type=jnp.float32
+            )
+            sums[:rows, h * quarter : (h + 1) * quarter] += both_parts[:rows] + both_parts[rows:]
+        return carry
+
+    lax.fori_loop(0, far, mix, 0)
+    mixed[...] = sums[:rows, :].astype(jnp.bfloat16)
 
     def settle(d, carry):
         other = lax.rem(me + d, members)
-        back_copy(other, other).wait_recv()
         back_copy(other, me).wait_send()
         row_copy(other, me).wait_send()
         return carry
@@ -467,12 +516,12 @@
     lax.fori_loop(0, chunks, drain, 0)
 
 
-def layer(resid, context, out_weight, gain, pick, gate_up, down_weight):
+def layer(resid, context, out_weight, gain, order, expert_ids, slots, combine, gate_up, down_weight):
     members = lax.axis_size("expert")
     far = members // near
     rows, half = resid.shape
     depth = out_weight.shape[0]
-    slot_rows = pick.shape[0]
+    slot_rows = order.shape[0]
     width, ffe = gate_up.shape[2:]
     dma = pltpu.SemaphoreType.DMA
     vmem = pl.BlockSpec(memory_space=pltpu.VMEM)
@@ -480,12 +529,9 @@
     wire = jnp.bfloat16
     return pl.pallas_call(
         functools.partial(layer_kernel, members),
-        out_shape=[
-            jax.ShapeDtypeStruct((rows, half), wire),
-            jax.ShapeDtypeStruct((slot_rows, half // 2), wire),
-        ],
-        in_specs=[vmem] * 5 + [far_spec] * 2,
-        out_specs=[vmem, vmem],
+        out_shape=jax.ShapeDtypeStruct((rows, half), wire),
+        in_specs=[vmem] + [far_spec] * 2 + [vmem] * 5 + [far_spec] * 2,
+        out_specs=vmem,
         scratch_shapes=[
             pltpu.VMEM((near * depth, half), wire),
             pltpu.VMEM((far * rows, near * depth), wire),
@@ -499,6 +545,10 @@
             pltpu.VMEM((2 * ffe, half), wire),
             pltpu.VMEM((slot_rows // 2, 2 * ffe), wire),
             pltpu.VMEM((slot_rows, half // 2), wire),
+            pltpu.VMEM((rows, half), wire),
+            pltpu.VMEM((slot_rows, half // 2), wire),
+            pltpu.VMEM((slot_rows, 2 * rows), wire),
+            pltpu.VMEM((far, 2, 2 * rows, slot_rows // far), wire),
             dma((7,)),
             dma((near, chunks)),
             dma((near, chunks)),
@@ -524,7 +574,7 @@
             collective_id=0, has_side_effects=True, vmem_limit_bytes=60 * 2**20
         ),
         name="layer",
-    )(resid, context, out_weight, gain, pick, gate_up, down_weight)
+    )(resid, context, out_weight, gain, order, expert_ids, slots, combine, gate_up, down_weight)
 
 
 def per_device(
@@ -541,30 +591,20 @@
 ):
     tok_rows, half_width = resid.shape
     members, capacity = token_order.shape
-    halves = jnp.arange(2, dtype=jnp.int32)
-    tokens = jnp.arange(tok_rows, dtype=jnp.int32)
-    pick = (token_order[:, None, :, None, None] == tokens) & (
-        halves[None, :, None, None, None] == halves[None, None, None, :, None]
+    halves = jnp.arange(2, dtype=jnp.int32)[None, :, None] * tok_rows
+    order = jnp.where(token_order[:, None, :] >= 0, token_order[:, None, :] + halves, -1)
+    return layer(
+        resid,
+        context,
+        out_weight,
+        norm_gain.reshape(1, 2 * half_width),
+        order.reshape(members * 2 * capacity, 1),
+        expert_ids,
+        slots,
+        combine,
+        gate_up,
+        down_weight,
     )
-    pick = pick.astype(jnp.bfloat16).reshape(members * 2 * capacity, 2 * tok_rows)
-    hidden_state, table = layer(
-        resid, context, out_weight, norm_gain.reshape(2, half_width), pick, gate_up, down_weight
-    )
-    flat_index = jnp.where(slots >= 0, (expert_ids * 2) * capacity + slots, -1)
-    places = jnp.arange(members * 2 * capacity, dtype=jnp.int32)
-    sums = []
-    for h in range(2):
-        weights = jnp.zeros((tok_rows, members * 2 * capacity), jnp.float32)
-        for column in range(expert_ids.shape[1]):
-            match = (flat_index[:, column, None] + h * capacity == places[None, :]) & (slots[:, column, None] >= 0)
-            weights = weights + jnp.where(match, combine[:, column, None], 0.0)
-        high = lax.reduce_precision(weights, 8, 7)
-        low = lax.reduce_precision(weights - high, 8, 7)
-        two = jnp.concatenate([high, low], axis=0).astype(jnp.bfloat16)
-        total = jnp.dot(two, table, preferred_element_type=jnp.float32)
-        sums.append(total[:tok_rows] + total[tok_rows:])
-    mixed_sum = jnp.concatenate(sums, axis=1)
-    return (hidden_state.astype(jnp.float32) + mixed_sum).astype(jnp.bfloat16)
 
 
 def solution(mesh):

time: 184 us -> 176 us (0.957)
  other arithmetic: 10.4 us -> 1.47 us
  matrix products: 3.07 us -> 0 us
  local copies, waits for them, and re-layouts: 4.32 us -> 7.34 us
    unnamed x4, local copies, waits for them, and re-layouts: 0.77 us -> 6.42 us
    another operation x4 -> x0, other arithmetic: 5.46 us -> none
    dot_general x2 -> x0, matrix products: 3.07 us -> none  [per_device(): total = jnp.dot(two, table, preferred_element_type=jnp.float32)]
    convert_element_type x2 -> x0, other arithmetic: 2.05 us -> none  [the longest x1 1.06 us: per_device(): return (hidden_state.astype(jnp.float32) + mixed_sum).astype(jnp.bfloat16)]
where the time goes in v4:
time: 176 us; the launch traced here: 175 us
  Pallas kernels  167 us (95%)
  local copies, waits for them, and re-layouts  7.34 us (4%)
    pallas_call x1, Pallas kernels, layer(): pl.pallas_call(functools.partial(layer_kernel, members), out_shape=jax.Sh...  167 us
    unnamed x4, local copies, waits for them, and re-layouts  6.42 us

profile of v4, /device:TPU:7, one launch (start us, length us, event | category | flops | bytes accessed | tf_op | source)
XLA Modules:
  0.0 175.4 jit_solution(17818155491025947493)
XLA Ops:
  0.0 0.7 broadcast_compare_fusion
  0.7 0.8 add_select_fusion
  1.5 1.4 copy.15.expert_ids
  2.9 1.4 copy.16.slots
  4.4 1.4 copy.17.combine
  5.8 0.9 select_n.16.order
  6.7 166.6 %layer.1 = bf16[192,2048]{1,0:T(8,128)(2,1)} custom-call(bf16[192,2048]{1,0:T(8,128)(2,1)} %resid.1, bf16[192,4096]{1,0:T(8,128)(2,1)} %context.1, bf16[256,2048]{1,0:T(8,128)(2,1)} %weight.1, f32[1,4096]{1,0:T(1,128)} %bitcast.1, s32[768,1]{1,0:T(8,128)} %select_n.16.order, s32[192,8]{1,0:T(8,128)} %copy.15.expert_ids, s32[192,8]{1,0:T(8,128)} %copy.16.slots, ...), custom_call_target="tpu_custom_call" | custom-call | tf_op jit(solution)/shard_map/layer/pallas_call | solution.py:530
  173.3 2.1 %copy.19 = bf16[192,2048]{1,0:T(8,128)(2,1)} copy(bf16[192,2048]{1,0:T(8,128)(2,1)} %layer.1) | data formatting | bytes 1572864
  (1 shorter events, 0.0 us)

commit v5 on v4

--- a/solution.py
+++ b/solution.py
@@ -19,9 +19,7 @@
     weight,
     gain,
     order,
-    expert_ids,
-    slots,
-    combine,
+    choices,
     gate_up,
     down_weight,
     mixed,
@@ -92,6 +90,24 @@
             device_id_type=pl.DeviceIdType.MESH,
         )
 
+    def corner_copy(c):
+        d = 1 + lax.rem(c, 2)
+        owner = lax.bitwise_xor(spot, 3 - d)
+        place = plane_weight.at[pl.ds(pl.multiple_of(owner * depth, depth), depth), columns(c)]
+        return pltpu.make_async_remote_copy(
+            src_ref=place,
+            dst_ref=place,
+            send_sem=weight_send.at[3, c],
+            recv_sem=weight_recv.at[3, c],
+            device_id={"expert": line * near + lax.bitwise_xor(spot, d)},
+            device_id_type=pl.DeviceIdType.MESH,
+        )
+
+    def hand_on(c):
+        weight_copy(1, c).wait_recv()
+        weight_copy(2, c).wait_recv()
+        corner_copy(c).start()
+
     def context_copy(d):
         target = lax.rem(line + d, far)
         return pltpu.make_async_remote_copy(
@@ -161,7 +177,7 @@
     for d in range(1, far):
         context_copy(d).start()
     for c in range(chunks):
-        for d in (3, 1, 2):
+        for d in (1, 2):
             weight_copy(d, c).start()
     ffe = gate_up.shape[3]
     loads = [
@@ -180,8 +196,11 @@
         share_copy(d).start()
 
     def multiply(c):
-        for d in range(1, near):
-            weight_copy(d, c).wait_recv()
+        @pl.when(c + 1 < chunks)
+        def _():
+            hand_on(c + 1)
+
+        corner_copy(c).wait_recv()
 
         def block(k, carry):
             q = lax.select(line * 2 < far, far - 1 - k, k)
@@ -249,6 +268,7 @@
 
         return carry
 
+    hand_on(0)
     lax.fori_loop(0, chunks, step, 0)
     forward(chunks - 1)
 
@@ -371,13 +391,15 @@
 
     lax.fori_loop(0, far, dispatch, 0)
     def weigh(q, carry):
-        flat = expert_ids[...] * both + slots[...] - q * near * both
-        live = slots[...] >= 0
-        share = jnp.where(live, combine[...], 0.0)
+        top = choices.shape[1] // 2
+        flat = choices[:, :top].astype(jnp.int32)
+        live = flat >= 0
+        flat = flat - q * near * both
+        share = choices[:, top:]
         for h in range(2):
             place = lax.broadcasted_iota(jnp.int32, (rows, near * both), 1) - h * cap
             total = jnp.zeros((rows, near * both), jnp.float32)
-            for k in range(expert_ids.shape[1]):
+            for k in range(top):
                 same = live[:, k : k + 1] & (flat[:, k : k + 1] == place)
                 total = total + jnp.where(same, share[:, k : k + 1], 0.0)
             high = total.astype(jnp.bfloat16)
@@ -498,8 +520,9 @@
         share_copy(d).wait_send()
 
     def drain(c, carry):
-        for d in range(1, near):
+        for d in range(1, near - 1):
             weight_copy(d, c).wait_send()
+        corner_copy(c).wait_send()
 
         def right_done(q, inner):
             right_copy(q, c).wait_send()
@@ -516,7 +539,7 @@
     lax.fori_loop(0, chunks, drain, 0)
 
 
-def layer(resid, context, out_weight, gain, order, expert_ids, slots, combine, gate_up, down_weight):
+def layer(resid, context, out_weight, gain, order, choices, gate_up, down_weight):
     members = lax.axis_size("expert")
     far = members // near
     rows, half = resid.shape
@@ -530,7 +553,7 @@
     return pl.pallas_call(
         functools.partial(layer_kernel, members),
         out_shape=jax.ShapeDtypeStruct((rows, half), wire),
-        in_specs=[vmem] + [far_spec] * 2 + [vmem] * 5 + [far_spec] * 2,
+        in_specs=[vmem] + [far_spec] * 2 + [vmem] * 3 + [far_spec] * 2,
         out_specs=vmem,
         scratch_shapes=[
             pltpu.VMEM((near * depth, half), wire),
@@ -574,7 +597,7 @@
             collective_id=0, has_side_effects=True, vmem_limit_bytes=60 * 2**20
         ),
         name="layer",
-    )(resid, context, out_weight, gain, order, expert_ids, slots, combine, gate_up, down_weight)
+    )(resid, context, out_weight, gain, order, choices, gate_up, down_weight)
 
 
 def per_device(
@@ -593,15 +616,16 @@
     members, capacity = token_order.shape
     halves = jnp.arange(2, dtype=jnp.int32)[None, :, None] * tok_rows
     order = jnp.where(token_order[:, None, :] >= 0, token_order[:, None, :] + halves, -1)
+    live = slots >= 0
+    place = jnp.where(live, expert_ids * (2 * capacity) + slots, -1).astype(jnp.float32)
+    choices = jnp.concatenate([place, jnp.where(live, combine, 0.0)], axis=1)
     return layer(
         resid,
         context,
         out_weight,
         norm_gain.reshape(1, 2 * half_width),
         order.reshape(members * 2 * capacity, 1),
-        expert_ids,
-        slots,
-        combine,
+        choices,
         gate_up,
         down_weight,
     )

time: 176 us -> 182 us (1.034)
  Pallas kernels: 167 us -> 175 us
  local copies, waits for them, and re-layouts: 7.34 us -> 3.74 us
    pallas_call x1, Pallas kernels: 167 us -> 175 us  [layer(): pl.pallas_call(functools.partial(layer_kernel, members), out_shape=jax.Sh...]
    unnamed x4 -> x1, local copies, waits for them, and re-layouts: 6.42 us -> 2.09 us
where the time goes in v5:
time: 182 us; the launch traced here: 181 us
  Pallas kernels  175 us (96%)
  local copies, waits for them, and re-layouts  3.74 us (2%)
  other arithmetic  2.92 us (2%)
    pallas_call x1, Pallas kernels, layer(): pl.pallas_call(functools.partial(layer_kernel, members), out_shape=jax.Sh...  175 us

profile of v5, /device:TPU:7, one launch (start us, length us, event | category | flops | bytes accessed | tf_op | source)
XLA Modules:
  0.0 181.4 jit_solution(7829019878279977332)
XLA Ops:
  0.0 0.7 broadcast_compare_fusion.1
  0.7 0.7 select_convert_fusion
  1.4 0.7 broadcast_select_fusion
  2.1 0.8 add_select_fusion
  2.9 0.7 copy.27.choices
  3.7 0.9 select_n.26.order
  4.6 174.7 %layer.1 = bf16[192,2048]{1,0:T(8,128)(2,1)} custom-call(bf16[192,2048]{1,0:T(8,128)(2,1)} %resid.1, bf16[192,4096]{1,0:T(8,128)(2,1)} %context.1, bf16[256,2048]{1,0:T(8,128)(2,1)} %weight.1, f32[1,4096]{1,0:T(1,128)} %bitcast.1, s32[768,1]{1,0:T(8,128)} %select_n.26.order, f32[192,16]{1,0:T(8,128)} %copy.27.choices, bf16[1,2,4096,384]{3,2,1,0:T(8,128)(2,1)} %gate_up.1, ...), custom_call_target="tpu_custom_call" | custom-call | tf_op jit(solution)/shard_map/layer/pallas_call | solution.py:553
  179.3 2.1 %copy.29 = bf16[192,2048]{1,0:T(8,128)(2,1)} copy(bf16[192,2048]{1,0:T(8,128)(2,1)} %layer.1) | data formatting | bytes 1572864
  (2 shorter events, 0.0 us)

commit v6 on v4

--- a/solution.py
+++ b/solution.py
@@ -19,9 +19,7 @@
     weight,
     gain,
     order,
-    expert_ids,
-    slots,
-    combine,
+    choices,
     gate_up,
     down_weight,
     mixed,
@@ -371,13 +369,15 @@
 
     lax.fori_loop(0, far, dispatch, 0)
     def weigh(q, carry):
-        flat = expert_ids[...] * both + slots[...] - q * near * both
-        live = slots[...] >= 0
-        share = jnp.where(live, combine[...], 0.0)
+        top = choices.shape[1] // 2
+        flat = choices[:, :top].astype(jnp.int32)
+        live = flat >= 0
+        flat = flat - q * near * both
+        share = choices[:, top:]
         for h in range(2):
             place = lax.broadcasted_iota(jnp.int32, (rows, near * both), 1) - h * cap
             total = jnp.zeros((rows, near * both), jnp.float32)
-            for k in range(expert_ids.shape[1]):
+            for k in range(top):
                 same = live[:, k : k + 1] & (flat[:, k : k + 1] == place)
                 total = total + jnp.where(same, share[:, k : k + 1], 0.0)
             high = total.astype(jnp.bfloat16)
@@ -516,7 +516,7 @@
     lax.fori_loop(0, chunks, drain, 0)
 
 
-def layer(resid, context, out_weight, gain, order, expert_ids, slots, combine, gate_up, down_weight):
+def layer(resid, context, out_weight, gain, order, choices, gate_up, down_weight):
     members = lax.axis_size("expert")
     far = members // near
     rows, half = resid.shape
@@ -530,7 +530,7 @@
     return pl.pallas_call(
         functools.partial(layer_kernel, members),
         out_shape=jax.ShapeDtypeStruct((rows, half), wire),
-        in_specs=[vmem] + [far_spec] * 2 + [vmem] * 5 + [far_spec] * 2,
+        in_specs=[vmem] + [far_spec] * 2 + [vmem] * 3 + [far_spec] * 2,
         out_specs=vmem,
         scratch_shapes=[
             pltpu.VMEM((near * depth, half), wire),
@@ -574,7 +574,7 @@
             collective_id=0, has_side_effects=True, vmem_limit_bytes=60 * 2**20
         ),
         name="layer",
-    )(resid, context, out_weight, gain, order, expert_ids, slots, combine, gate_up, down_weight)
+    )(resid, context, out_weight, gain, order, choices, gate_up, down_weight)
 
 
 def per_device(
@@ -593,15 +593,16 @@
     members, capacity = token_order.shape
     halves = jnp.arange(2, dtype=jnp.int32)[None, :, None] * tok_rows
     order = jnp.where(token_order[:, None, :] >= 0, token_order[:, None, :] + halves, -1)
+    live = slots >= 0
+    place = jnp.where(live, expert_ids * (2 * capacity) + slots, -1).astype(jnp.float32)
+    choices = jnp.concatenate([place, jnp.where(live, combine, 0.0)], axis=1)
     return layer(
         resid,
         context,
         out_weight,
         norm_gain.reshape(1, 2 * half_width),
         order.reshape(members * 2 * capacity, 1),
-        expert_ids,
-        slots,
-        combine,
+        choices,
         gate_up,
         down_weight,
     )

time: 176 us -> 174 us (0.989)
  local copies, waits for them, and re-layouts: 7.34 us -> 3.74 us
    unnamed x4 -> x1, local copies, waits for them, and re-layouts: 6.42 us -> 2.09 us
where the time goes in v6:
time: 174 us; the launch traced here: 173 us
  Pallas kernels  166 us (95%)
  local copies, waits for them, and re-layouts  3.74 us (2%)
  other arithmetic  2.92 us (2%)
    pallas_call x1, Pallas kernels, layer(): pl.pallas_call(functools.partial(layer_kernel, members), out_shape=jax.Sh...  166 us

profile of v6, /device:TPU:7, one launch (start us, length us, event | category | flops | bytes accessed | tf_op | source)
XLA Modules:
  0.0 173.1 jit_solution(559963852738505323)
XLA Ops:
  0.0 0.7 broadcast_compare_fusion.1
  0.7 0.7 select_convert_fusion
  1.4 0.7 broadcast_select_fusion
  2.1 0.8 add_select_fusion
  2.9 0.7 copy.27.choices
  3.7 0.9 select_n.26.order
  4.6 166.5 %layer.1 = bf16[192,2048]{1,0:T(8,128)(2,1)} custom-call(bf16[192,2048]{1,0:T(8,128)(2,1)} %resid.1, bf16[192,4096]{1,0:T(8,128)(2,1)} %context.1, bf16[256,2048]{1,0:T(8,128)(2,1)} %weight.1, f32[1,4096]{1,0:T(1,128)} %bitcast.1, s32[768,1]{1,0:T(8,128)} %select_n.26.order, f32[192,16]{1,0:T(8,128)} %copy.27.choices, bf16[1,2,4096,384]{3,2,1,0:T(8,128)(2,1)} %gate_up.1, ...), custom_call_target="tpu_custom_call" | custom-call | tf_op jit(solution)/shard_map/layer/pallas_call | solution.py:530
  171.1 2.1 %copy.29 = bf16[192,2048]{1,0:T(8,128)(2,1)} copy(bf16[192,2048]{1,0:T(8,128)(2,1)} %layer.1) | data formatting | bytes 1572864
  (2 shorter events, 0.0 us)
